TPU v7x, 256 devices: a whole 4x4x8 slice. The times are simulated.
256 devices in a mesh: freq: 32 (over z_lo, y, x), band: 8 (over z_hi, core).
Axes of the slice: x: 4, y: 4, z: 8 (z_hi: 4, z_lo: 2; z = z_hi * 2 + z_lo), core: 2. Of those that a mesh axis runs over, the one named last changes fastest.
Arguments:
- wavefields: float32 [32, 4, 1024, 1024], P('freq', None, None, 'band'), may hold values from -6 to 6
- slowness_store: float32 [32, 1024, 1024], P('freq', None, 'band'), may hold values from 0.8 to 1.25
- owner_plan: int32 [3], replicated, may hold values from 0 to 31
- freq_slot: int32 [32], P('freq'), may hold values from 0 to 31, as said below
Outputs:
- migrated_image: float32 [3, 1024, 1024], P(None, 'freq', 'band')
- bottom_fields: float32 [32, 4, 1024, 1024], P('freq', None, None, 'band')
Inputs may be any that keep to these rules, and one draw needn't show every extreme that they name: `freq_slot`: every frequency number appears once.
All inputs are finite; a program needn't handle non-finite values.
Results may differ from a plain program's by a relative error of at most 0.034.
Values may be sent and summed in bfloat16 or wider, within the bound.
A program may use at most 128 MiB of HBM per device.

v0:
```python
import math

import jax
import jax.numpy as jnp
from jax import lax
from jax.sharding import PartitionSpec as P

OMEGA_LO = 1.5
OMEGA_HI = 3.0


def from_root(block, axis, owner):
    block = jnp.where(lax.axis_index(axis) == owner, block, jnp.zeros_like(block))
    return lax.psum(block, axis)


def sine_table(length):
    ordinal = jnp.arange(1, length + 1, dtype=jnp.int32)
    modulo = ordinal[:, None] * ordinal[None, :] % (2 * (length + 1))
    angles = math.pi * modulo.astype(jnp.float32) / (length + 1)
    return (math.sqrt(2.0 / (length + 1)) * jnp.sin(angles)).astype(jnp.bfloat16)


def wavenumbers(length, first, total):
    ordinal = first + jnp.arange(1, length + 1, dtype=jnp.int32)
    return math.pi * ordinal.astype(jnp.float32) / (total + 1)


def spectral_factors(omega_value, wave_rows, wave_columns):
    squared = (
        omega_value * omega_value
        - wave_rows[:, None] * wave_rows[:, None]
        - wave_columns[None, :] * wave_columns[None, :]
    )
    vertical = jnp.sqrt(jnp.maximum(squared, 0.0))
    decay = jnp.sqrt(jnp.maximum(-squared, 0.0))
    return (jnp.cos(vertical), jnp.sin(vertical), jnp.exp(-decay))


def rotate(fields, cosine, sine_part, damping):
    pieces = []
    for offset, handed in ((0, -1.0), (2, 1.0)):
        real_part = fields[offset]
        imag_part = fields[offset + 1]
        pieces.append(damping * (real_part * cosine - handed * imag_part * sine_part))
        pieces.append(damping * (imag_part * cosine + handed * real_part * sine_part))
    return jnp.stack(pieces)


def body(wavefields, slowness_store, owner_plan, freq_slot):
    fields = wavefields[0]
    lateral = fields.shape[1]
    band_rows = fields.shape[2]
    band_count = lax.axis_size("band")
    freq_count = lax.axis_size("freq")
    total_rows = band_rows * band_count
    strip = lateral // band_count
    depth_count = owner_plan.shape[0]
    lateral_table = sine_table(lateral)
    band_table = sine_table(total_rows)
    wave_rows = wavenumbers(strip, lax.axis_index("band") * strip, lateral)
    wave_columns = wavenumbers(total_rows, 0, total_rows)
    omega_value = (
        OMEGA_LO + (OMEGA_HI - OMEGA_LO) * (freq_slot[0].astype(jnp.float32) + 0.5) / freq_count
    )
    cosine_k, sine_k, damping_k = spectral_factors(omega_value, wave_rows, wave_columns)
    normalizer = 1.0 / math.sqrt(freq_count)
    own_slab = slowness_store[0]
    pieces_done = []
    for layer_index in range(depth_count):
        slowness = from_root(own_slab, "freq", owner_plan[layer_index])
        split_phase = omega_value * (slowness - 1.0)
        shifted = rotate(fields, jnp.cos(split_phase), jnp.sin(split_phase), 1.0).astype(
            jnp.bfloat16
        )
        half_spectrum = jnp.einsum(
            "kx,cxy->cky", lateral_table, shifted, preferred_element_type=jnp.float32
        ).astype(jnp.bfloat16)
        line_spectrum = lax.all_to_all(
            half_spectrum, "band", split_axis=1, concat_axis=2, tiled=True
        )
        spectrum = jnp.einsum(
            "cky,ly->ckl", line_spectrum, band_table, preferred_element_type=jnp.float32
        )
        turned = rotate(spectrum, cosine_k, sine_k, damping_k).astype(jnp.bfloat16)
        partial_back = jnp.einsum(
            "ckl,ly->cky", turned, band_table, preferred_element_type=jnp.float32
        ).astype(jnp.bfloat16)
        row_back = lax.all_to_all(partial_back, "band", split_axis=2, concat_axis=1, tiled=True)
        fields = jnp.einsum(
            "kx,cky->cxy", lateral_table, row_back, preferred_element_type=jnp.float32
        )
        partial_value = (fields[0] * fields[2] + fields[1] * fields[3]) * normalizer
        pieces_done.append(
            lax.psum_scatter(
                partial_value.astype(jnp.bfloat16), "freq", scatter_dimension=0, tiled=True
            ).astype(jnp.float32)
        )
    image_sum = jnp.stack(pieces_done)
    return (image_sum, fields[None])


def solution(mesh):
    in_specs = (P("freq", None, None, "band"), P("freq", None, "band"), P(), P("freq"))
    out_specs = (P(None, "freq", "band"), P("freq", None, None, "band"))
    return jax.shard_map(body, mesh=mesh, in_specs=in_specs, out_specs=out_specs, check_vma=False)
```

profile of v0, /device:TPU:32, one launch (start us, length us, event | category | flops | bytes accessed | tf_op | source)
XLA Modules:
  0.0 1214.7 jit_solution(8065579839549878748)
XLA Ops:
  7.2 1.4 fusion.298
  10.6 1.2 copy.22
  11.9 1.2 select_bitcast_fusion
  14.0 1.1 fusion.297
  15.2 1.2 copy.51
  16.4 1.2 copy.52
  18.1 313.5 %all-reduce.3.cloned.1.call-done = (f32[1024,128]{0,1:T(8,128)}, f32[1024,128]{0,1:T(8,128)}, f32[1024,128]{0,1:T(8,128)}) async-done(((f32[1024,128]{0,1:T(8,128)}, f32[1024,128]{0,1:T(8,128)}, f32[1024,128]{0,1:T(8,128)}), (f32[1024,128]{0,1:T(8,128)}, f32[1024,128]{0,1:T(8,128)}, f32[1024,128]{0,1:T(8,128)})) %all-reduce.3.cloned.1.call-update) | async-done | bytes 1572880 | tf_op jit(solution)/shard_map/psum | solution.py:14
  331.6 3.5 fusion.239
  335.0 16.7 %fusion.99 = bf16[4,1024,128]{1,2,0:T(8,128)(2,1)S(1)} fusion(s32[1024]{0:T(1024)S(1)} %iota_add_fusion, bf16[1,1024,128]{1,2,0:T(8,128)(2,1)S(1)} %get-tuple-element.39, bf16[1,1024,128]{1,2,0:T(8,128)(2,1)S(1)} %get-tuple-element.40, bf16[1,1024,128]{1,2,0:T(8,128)(2,1)S(1)} %get-tuple-element.36, bf16[1,1024,128]{1,2,0:T(8,128)(2,1)S(1)} %get-tuple-element.35), kind=kOutput, calls=%fused_computation.69 | convolution fusion | flops 1087373312 | bytes 2101248 | tf_op jit(solution)/shard_map/kx,cxy->cky/dot_general | solution.py:76
  351.8 1.4 copy.26
  353.2 7.1 all-to-all-start
  360.3 28.8 %all-to-all-done = bf16[4,1024,128]{2,0,1:T(4,128)(2,1)S(1)} async-done(((bf16[4,1024,128]{2,0,1:T(4,128)(2,1)}), bf16[4,1024,128]{2,0,1:T(4,128)(2,1)S(1)}, u32[]{:S(2)}, u32[]{:S(2)}) %all-to-all-start) | async-done | bytes 1048608 | tf_op jit(solution)/shard_map/all_to_all | solution.py:79
  389.8 0.9 all_to_all.81
  390.7 17.1 %fusion.29 = f32[4,128,1024]{2,1,0:T(8,128)S(1)} fusion(bf16[4,128,1024]{2,1,0:T(8,128)(2,1)S(1)} %all_to_all.81, s32[1024]{0:T(1024)S(1)} %iota_add_fusion), kind=kOutput, calls=%fused_computation.21 | convolution fusion | flops 1085276160 | bytes 3149824 | tf_op jit(solution)/shard_map/cky,ly->ckl/dot_general | solution.py:82
  407.8 2.9 fusion.160
  410.7 17.1 %fusion.78 = bf16[4,128,1024]{2,1,0:T(8,128)(2,1)S(1)} fusion(s32[1024]{0:T(1024)S(1)} %iota_add_fusion, bf16[1,128,1024]{2,1,0:T(8,128)(2,1)S(1)} %get-tuple-element.27, bf16[1,128,1024]{2,1,0:T(8,128)(2,1)S(1)} %get-tuple-element.26, bf16[1,128,1024]{2,1,0:T(8,128)(2,1)S(1)} %get-tuple-element.28, bf16[1,128,1024]{2,1,0:T(8,128)(2,1)S(1)} %get-tuple-element.25), kind=kOutput, calls=%fused_computation.62 | convolution fusion | flops 1087373312 | bytes 2101248 | tf_op jit(solution)/shard_map/ckl,ly->cky/dot_general | solution.py:86
  428.5 32.0 %all_to_all.108 = bf16[4,128,1024]{1,0,2:T(4,128)(2,1)S(1)} all-to-all(bf16[4,128,1024]{1,0,2:T(4,128)(2,1)S(1)} %copy.28), channel_id=1, replica_groups=mesh['freq'=32,'band'=8] {'band'}, dimensions={2} | all-to-all | bytes 2097152 | tf_op jit(solution)/shard_map/all_to_all | solution.py:89
  461.9 17.2 %fusion.69 = f32[4,1024,128]{1,2,0:T(8,128)S(1)} fusion(bf16[4,1024,128]{1,2,0:T(8,128)(2,1)S(1)} %all_to_all.85, s32[1024]{0:T(1024)S(1)} %iota_add_fusion), kind=kOutput, calls=%fused_computation.59 | convolution fusion | flops 1085276160 | bytes 3149824 | tf_op jit(solution)/shard_map/kx,cky->cxy/dot_general | solution.py:90
  479.1 2.3 fusion.230
  481.4 16.7 %fusion.96 = bf16[4,1024,128]{1,2,0:T(8,128)(2,1)S(1)} fusion(s32[1024]{0:T(1024)S(1)} %iota_add_fusion, bf16[1,1024,128]{1,2,0:T(8,128)(2,1)S(1)} %get-tuple-element.15, bf16[1,1024,128]{1,2,0:T(8,128)(2,1)S(1)} %get-tuple-element.16, bf16[1,1024,128]{1,2,0:T(8,128)(2,1)S(1)} %get-tuple-element.14, bf16[1,1024,128]{1,2,0:T(8,128)(2,1)S(1)} %get-tuple-element.13), kind=kOutput, calls=%fused_computation.68 | convolution fusion | flops 1087373312 | bytes 2101248 | tf_op jit(solution)/shard_map/kx,cxy->cky/dot_general | solution.py:76
  498.9 31.0 %all_to_all.109 = bf16[4,1024,128]{2,0,1:T(4,128)(2,1)S(1)} all-to-all(bf16[4,1024,128]{2,0,1:T(4,128)(2,1)S(1)} %copy.31), channel_id=1, replica_groups=mesh['freq'=32,'band'=8] {'band'}, dimensions={1} | all-to-all | bytes 2097152 | tf_op jit(solution)/shard_map/all_to_all | solution.py:79
  530.6 0.9 all_to_all.89
  531.5 17.1 %fusion.21 = f32[4,128,1024]{2,1,0:T(8,128)S(1)} fusion(bf16[4,128,1024]{2,1,0:T(8,128)(2,1)S(1)} %all_to_all.89, s32[1024]{0:T(1024)S(1)} %iota_add_fusion), kind=kOutput, calls=%fused_computation.17 | convolution fusion | flops 1085276160 | bytes 3149824 | tf_op jit(solution)/shard_map/cky,ly->ckl/dot_general | solution.py:82
  548.6 2.9 fusion.164
  551.4 17.1 %fusion.84 = bf16[4,128,1024]{2,1,0:T(8,128)(2,1)S(1)} fusion(s32[1024]{0:T(1024)S(1)} %iota_add_fusion, bf16[1,128,1024]{2,1,0:T(8,128)(2,1)S(1)} %get-tuple-element.23, bf16[1,128,1024]{2,1,0:T(8,128)(2,1)S(1)} %get-tuple-element.22, bf16[1,128,1024]{2,1,0:T(8,128)(2,1)S(1)} %get-tuple-element.24, bf16[1,128,1024]{2,1,0:T(8,128)(2,1)S(1)} %get-tuple-element.21), kind=kOutput, calls=%fused_computation.64 | convolution fusion | flops 1087373312 | bytes 2101248 | tf_op jit(solution)/shard_map/ckl,ly->cky/dot_general | solution.py:86
  569.3 31.3 %all_to_all.110 = bf16[4,128,1024]{1,0,2:T(4,128)(2,1)S(1)} all-to-all(bf16[4,128,1024]{1,0,2:T(4,128)(2,1)S(1)} %copy.33), channel_id=1, replica_groups=mesh['freq'=32,'band'=8] {'band'}, dimensions={2} | all-to-all | bytes 2097152 | tf_op jit(solution)/shard_map/all_to_all | solution.py:89
  601.9 17.2 %fusion.72 = f32[4,1024,128]{1,2,0:T(8,128)S(1)} fusion(bf16[4,1024,128]{1,2,0:T(8,128)(2,1)S(1)} %all_to_all.93, s32[1024]{0:T(1024)S(1)} %iota_add_fusion), kind=kOutput, calls=%fused_computation.60 | convolution fusion | flops 1085276160 | bytes 3149824 | tf_op jit(solution)/shard_map/kx,cky->cxy/dot_general | solution.py:90
  619.1 2.3 fusion.234
  621.4 16.7 %fusion.93 = bf16[4,1024,128]{1,2,0:T(8,128)(2,1)S(1)} fusion(s32[1024]{0:T(1024)S(1)} %iota_add_fusion, bf16[1,1024,128]{1,2,0:T(8,128)(2,1)S(1)} %get-tuple-element.11, bf16[1,1024,128]{1,2,0:T(8,128)(2,1)S(1)} %get-tuple-element.12, bf16[1,1024,128]{1,2,0:T(8,128)(2,1)S(1)} %get-tuple-element.10, bf16[1,1024,128]{1,2,0:T(8,128)(2,1)S(1)} %get-tuple-element.9), kind=kOutput, calls=%fused_computation.67 | convolution fusion | flops 1087373312 | bytes 2101248 | tf_op jit(solution)/shard_map/kx,cxy->cky/dot_general | solution.py:76
  638.9 32.4 %all_to_all.111 = bf16[4,1024,128]{2,0,1:T(4,128)(2,1)S(1)} all-to-all(bf16[4,1024,128]{2,0,1:T(4,128)(2,1)S(1)} %copy.36), channel_id=1, replica_groups=mesh['freq'=32,'band'=8] {'band'}, dimensions={1} | all-to-all | bytes 2097152 | tf_op jit(solution)/shard_map/all_to_all | solution.py:79
  672.0 0.9 all_to_all.97
  672.9 17.1 %fusion.13 = f32[4,128,1024]{2,1,0:T(8,128)S(1)} fusion(bf16[4,128,1024]{2,1,0:T(8,128)(2,1)S(1)} %all_to_all.97, s32[1024]{0:T(1024)S(1)} %iota_add_fusion), kind=kOutput, calls=%fused_computation.13 | convolution fusion | flops 1085276160 | bytes 3149824 | tf_op jit(solution)/shard_map/cky,ly->ckl/dot_general | solution.py:82
  690.0 2.9 fusion.168
  692.9 17.1 %fusion.90 = bf16[4,128,1024]{2,1,0:T(8,128)(2,1)S(1)} fusion(s32[1024]{0:T(1024)S(1)} %iota_add_fusion, bf16[1,128,1024]{2,1,0:T(8,128)(2,1)S(1)} %get-tuple-element.19, bf16[1,128,1024]{2,1,0:T(8,128)(2,1)S(1)} %get-tuple-element.18, bf16[1,128,1024]{2,1,0:T(8,128)(2,1)S(1)} %get-tuple-element.20, bf16[1,128,1024]{2,1,0:T(8,128)(2,1)S(1)} %get-tuple-element.17), kind=kOutput, calls=%fused_computation.66 | convolution fusion | flops 1087373312 | bytes 2101248 | tf_op jit(solution)/shard_map/ckl,ly->cky/dot_general | solution.py:86
  710.0 1.4 copy.38
  711.4 3.6 all-to-all-start.5
  715.0 0.8 copy.44
  716.0 0.8 copy.46
  716.9 27.2 %all-to-all-done.5 = bf16[4,128,1024]{1,0,2:T(4,128)(2,1)S(1)} async-done(((bf16[4,128,1024]{1,0,2:T(4,128)(2,1)}), bf16[4,128,1024]{1,0,2:T(4,128)(2,1)S(1)}, u32[]{:S(2)}, u32[]{:S(2)}) %all-to-all-start.5) | async-done | bytes 1048608 | tf_op jit(solution)/shard_map/all_to_all | solution.py:89
  745.5 16.6 %fusion.9 = f32[4,128,1024]{2,1,0:T(8,128)S(1)} fusion(bf16[4,1024,128]{1,2,0:T(8,128)(2,1)S(1)} %all_to_all.101, s32[1024]{0:T(1024)S(1)} %iota_add_fusion), kind=kOutput, calls=%fused_computation.11 | convolution fusion | flops 1085276160 | bytes 3149824 | tf_op jit(solution)/shard_map/kx,cky->cxy/dot_general | solution.py:90
  762.3 0.8 copy.48
  763.2 118.4 %reduce-scatter.10.cloned.1.call-done = bf16[32,128]{1,0:T(8,128)(2,1)} async-done(((bf16[1024,128]{1,0:T(8,128)(2,1)}), bf16[32,128]{1,0:T(8,128)(2,1)}) %reduce-scatter.10.cloned.1.call-update) | async-done | bytes 8208
  881.6 0.8 copy.45
  882.5 162.8 %reduce-scatter.12.cloned.1.call-done = bf16[32,128]{1,0:T(8,128)(2,1)} async-done(((bf16[1024,128]{1,0:T(8,128)(2,1)}), bf16[32,128]{1,0:T(8,128)(2,1)}) %reduce-scatter.12.cloned.1.call-update) | async-done | bytes 8208
  1045.3 0.8 copy.47
  1046.1 1.8 copy.43
  1048.0 158.5 %reduce-scatter.14.cloned.1.call-done = bf16[32,128]{1,0:T(8,128)(2,1)} async-done(((bf16[1024,128]{1,0:T(8,128)(2,1)}), bf16[32,128]{1,0:T(8,128)(2,1)}) %reduce-scatter.14.cloned.1.call-update) | async-done | bytes 8208
  1206.4 0.8 copy.49
  (37 shorter events, 11.0 us)
Async XLA Ops:
  7.2 324.4 %all-reduce.3.cloned.1.call-start = ((), (), s32[]{:S(2)}) async-start(), calls=%async_computation.12 | async-start | bytes 3145728 | tf_op jit(solution)/shard_map/psum | solution.py:14
  11.9 2.2 copy-start
  353.2 35.9 %all-to-all-start = ((bf16[4,1024,128]{2,0,1:T(4,128)(2,1)}), bf16[4,1024,128]{2,0,1:T(4,128)(2,1)S(1)}, u32[]{:S(2)}, u32[]{:S(2)}) async-start(bf16[4,1024,128]{2,0,1:T(4,128)(2,1)} %copy.26), calls=%async_computation | async-start | bytes 2097152 | tf_op jit(solution)/shard_map/all_to_all | solution.py:79
  461.9 17.2 %copy-start.2 = (f32[1024,128]{0,1:T(8,128)S(1)}, f32[1024,128]{0,1:T(8,128)}, u32[]{:S(2)}) copy-start(f32[1024,128]{0,1:T(8,128)} %get-tuple-element.7) | copy-start | bytes 1572868
  601.9 17.2 %copy-start.1 = (f32[1024,128]{0,1:T(8,128)S(1)}, f32[1024,128]{0,1:T(8,128)}, u32[]{:S(2)}) copy-start(f32[1024,128]{0,1:T(8,128)} %get-tuple-element.8) | copy-start | bytes 1572868
  711.4 32.7 %all-to-all-start.5 = ((bf16[4,128,1024]{1,0,2:T(4,128)(2,1)}), bf16[4,128,1024]{1,0,2:T(4,128)(2,1)S(1)}, u32[]{:S(2)}, u32[]{:S(2)}) async-start(bf16[4,128,1024]{1,0,2:T(4,128)(2,1)} %copy.38), calls=%async_computation.5 | async-start | bytes 2097152 | tf_op jit(solution)/shard_map/all_to_all | solution.py:89
  715.0 166.6 %reduce-scatter.10.cloned.1.call-start = ((), (), s32[]{:S(2)}) async-start(), calls=%async_computation.9 | async-start | bytes 270336
  715.9 329.4 %reduce-scatter.12.cloned.1.call-start = ((), (), s32[]{:S(2)}) async-start(), calls=%async_computation.10 | async-start | bytes 270336
  716.8 489.6 %reduce-scatter.14.cloned.1.call-start = ((), (), s32[]{:S(2)}) async-start(), calls=%async_computation.11 | async-start | bytes 270336
Sparse Core Ops, SparseCore 0:
  13.3 318.2 all-reduce.2
  718.5 163.0 reduce-scatter.9
  884.1 161.1 reduce-scatter.11
  1047.8 158.6 reduce-scatter.13
where the time goes:
time: 1230 us; the launch traced here: 1210 us
  waiting for transfers between devices  809 us (66%)
  matrix products  204 us (17%)
  blocking collectives  127 us (10%)
  local copies, waits for them, and re-layouts  28.6 us (2%)
  other arithmetic  18.8 us (2%)
  between operations  16.9 us (1%)
    unnamed x7, waiting for transfers between devices  440 us
    psum x1, waiting for transfers between devices, from_root(): return lax.psum(block, axis)  313 us
    all_to_all x2, blocking collectives, body(): lax.all_to_all(half_spectrum, 'band', split_axis=1, concat_axis=2, tiled=...  63.4 us
    all_to_all x2, blocking collectives, body(): lax.all_to_all(partial_back, 'band', split_axis=2, concat_axis=1, tiled=T...  63.3 us
    dot_general x3, matrix products, body(): jnp.einsum('cky,ly->ckl', line_spectrum, band_table, preferred_element_ty...  51.3 us
    dot_general x3, matrix products, body(): jnp.einsum('ckl,ly->cky', turned, band_table, preferred_element_type=jnp....  51.2 us
    dot_general x3, matrix products, body(): jnp.einsum('kx,cky->cxy', lateral_table, row_back, preferred_element_type...  51.1 us
    dot_general x3, matrix products, body(): jnp.einsum('kx,cxy->cky', lateral_table, shifted, preferred_element_type=...  50.1 us
  transfers between devices with their start and end apart: 6, of which 6 were waited for; matrix products, arithmetic and copies ran while one was open for 2% of the time, Pallas kernels for 0%

commit v1 on v0

v1 whole, which is shorter than its diff:
```python
import functools
import math

import jax
import jax.numpy as jnp
import numpy as np
from jax import lax
from jax.experimental import pallas as pl
from jax.experimental.pallas import tpu as pltpu
from jax.sharding import PartitionSpec as P

OMEGA_LO = 1.5
OMEGA_HI = 3.0
MESH = pl.DeviceIdType.MESH
BF16 = jnp.bfloat16
F32 = jnp.float32


def sine_table(length):
    ordinal = np.arange(1, length + 1, dtype=np.int64)
    modulo = ordinal[:, None] * ordinal[None, :] % (2 * (length + 1))
    angles = math.pi * modulo / (length + 1)
    return (math.sqrt(2.0 / (length + 1)) * np.sin(angles)).astype(np.float32).astype(BF16)


def small_cos_sin(phi):
    p2 = phi * phi
    cosine = 1.0 + p2 * (-1 / 2 + p2 * (1 / 24 + p2 * (-1 / 720 + p2 * (1 / 40320))))
    sine = phi * (1.0 + p2 * (-1 / 6 + p2 * (1 / 120 + p2 * (-1 / 5040 + p2 * (1 / 362880)))))
    return cosine, sine


def kernel(
    dims,
    owner,
    slot,
    table,
    slab,
    wave,
    image,
    bottom,
    fields,
    shifted,
    tx,
    rx,
    turned,
    ptx,
    prx,
    trig,
    factor,
    chunk_tx,
    chunk_rx,
    select,
    slow,
    image_tx,
    image_rx,
    load_sem,
    chunk_send,
    chunk_recv,
    slow_send,
    slow_recv,
    fwd_send,
    fwd_recv,
    back_send,
    back_recv,
    image_send,
    image_recv,
):
    freqs, bands, lateral, depth = dims
    strip = lateral // bands
    rows = lateral // freqs
    tile = min(256, lateral)
    tiles = lateral // tile
    per_tile = tile // strip
    f = lax.axis_index("freq")
    b = lax.axis_index("band")
    omega = OMEGA_LO + (OMEGA_HI - OMEGA_LO) * (slot[0].astype(F32) + 0.5) / freqs

    def wait_bytes(ref, sem):
        pltpu.make_async_copy(ref, ref, sem).wait()

    barrier = pltpu.get_barrier_semaphore()

    def greet_freq(d, carry):
        pl.semaphore_signal(
            barrier, inc=1, device_id={"freq": lax.rem(f + d, freqs)}, device_id_type=MESH
        )
        return carry

    def greet_band(d, carry):
        pl.semaphore_signal(
            barrier, inc=1, device_id={"band": lax.rem(b + d, bands)}, device_id_type=MESH
        )
        return carry

    lax.fori_loop(1, freqs, greet_freq, 0)
    lax.fori_loop(1, bands, greet_band, 0)
    loads = [
        pltpu.make_async_copy(
            wave.at[0, 2 * u + c], fields.at[u, :, pl.ds(c * strip, strip)], load_sem
        )
        for u in range(2)
        for c in range(2)
    ]
    for load in loads:
        load.start()
    chunk_tx[:, 0:rows, :] = (slab[0] - 1.0).astype(BF16).reshape(freqs, rows, strip)
    chunk_tx[:, rows:, :] = jnp.full((freqs, 16, strip), slot[0].astype(F32)).astype(BF16)
    pl.semaphore_wait(barrier, freqs + bands - 2)

    def send_chunk(d, carry):
        g = lax.rem(f + d, freqs)
        pltpu.make_async_remote_copy(
            chunk_tx.at[g],
            chunk_rx.at[f],
            chunk_send,
            chunk_recv,
            device_id={"freq": g},
            device_id_type=MESH,
        ).start()
        return carry

    lax.fori_loop(1, freqs, send_chunk, 0)
    pltpu.make_async_copy(chunk_tx.at[f], chunk_rx.at[f], chunk_recv).start()

    def make_factor(n, carry):
        lanes = pl.ds(pl.multiple_of(n * strip, strip), strip)
        shape = (strip, strip)
        kx = (lax.broadcasted_iota(jnp.int32, shape, 0) + (b * strip + 1)).astype(F32)
        ky = (lax.broadcasted_iota(jnp.int32, shape, 1) + (n * strip + 1)).astype(F32)
        kx = math.pi * kx / (lateral + 1)
        ky = math.pi * ky / (lateral + 1)
        q = omega * omega - kx * kx - ky * ky
        theta = jnp.sqrt(jnp.maximum(q, 0.0))
        damp = jnp.exp(-jnp.sqrt(jnp.maximum(-q, 0.0)))
        factor[0, :, lanes] = damp * jnp.cos(theta)
        factor[1, :, lanes] = damp * jnp.sin(theta)
        return carry

    lax.fori_loop(0, bands, make_factor, 0)

    wait_bytes(chunk_rx, chunk_recv)
    for z in range(depth):
        select[z] = chunk_rx[owner[z], 0:rows, :]

    def send_slow(first, count, sem):
        def body(d, carry):
            g = lax.rem(f + d, freqs)
            pltpu.make_async_remote_copy(
                select.at[pl.ds(first, count)],
                slow.at[pl.ds(first, count), f],
                slow_send.at[sem],
                slow_recv.at[sem],
                device_id={"freq": g},
                device_id_type=MESH,
            ).start()
            return carry

        lax.fori_loop(1, freqs, body, 0)
        pltpu.make_async_copy(
            select.at[pl.ds(first, count)], slow.at[pl.ds(first, count), f], slow_recv.at[sem]
        ).start()

    def make_trig(z):
        def body(g, carry):
            block = pl.ds(pl.multiple_of(g * rows, rows), rows)
            cosine, sine = small_cos_sin(omega * slow[z, g].astype(F32))
            trig[z, 0, block] = cosine
            trig[z, 1, block] = sine
            return carry

        lax.fori_loop(0, freqs, body, 0)

    send_slow(0, 1, 0)
    send_slow(1, depth - 1, 1)
    for load in loads:
        load.wait()
    wait_bytes(slow.at[0], slow_recv.at[0])
    make_trig(0)

    def hand(u):
        return -1.0 if u == 0 else 1.0

    def to_wavenumbers(z, u):
        def shift(i, carry):
            block = pl.ds(pl.multiple_of(i * strip, strip), strip)
            cosine = trig[z, 0, block]
            sine = trig[z, 1, block] * hand(u)
            re = fields[u, block, 0:strip]
            im = fields[u, block, strip:]
            shifted[u, block, 0:strip] = (re * cosine - im * sine).astype(BF16)
            shifted[u, block, strip:] = (im * cosine + re * sine).astype(BF16)
            return carry

        lax.fori_loop(0, bands, shift, 0)

        @pl.when(z > 0)
        def _():
            wait_bytes(tx.at[u, :, pl.ds(0, lateral - strip)], fwd_send.at[u])

        def product(i, carry):
            t = lax.rem(b // per_tile + 1 + i, tiles)
            block = pl.ds(pl.multiple_of(t * tile, tile), tile)
            half = jnp.dot(table[block, :], shifted[u], preferred_element_type=F32).astype(BF16)
            tx[u, 0, block] = half[:, 0:strip]
            tx[u, 1, block] = half[:, strip:]
            for p in range(per_tile):
                j = t * per_tile + p
                src = tx.at[u, :, pl.ds(pl.multiple_of(j * strip, strip), strip)]
                dst = rx.at[u, :, :, pl.ds(pl.multiple_of(b * strip, strip), strip)]

                @pl.when(j != b)
                def _():
                    pltpu.make_async_remote_copy(
                        src,
                        dst,
                        fwd_send.at[u],
                        fwd_recv.at[u],
                        device_id={"band": j},
                        device_id_type=MESH,
                    ).start()

                @pl.when(j == b)
                def _():
                    pltpu.make_async_copy(src, dst, fwd_recv.at[u]).start()

            return carry

        lax.fori_loop(0, tiles, product, 0)

    def turn(z, u):
        wait_bytes(rx.at[u], fwd_recv.at[u])

        def product(n, carry):
            lanes = pl.ds(pl.multiple_of(n * tile, tile), tile)
            lines = rx[u].reshape(2 * strip, lateral)
            spectrum = jnp.dot(lines, table[:, lanes], preferred_element_type=F32)
            re = spectrum[0:strip]
            im = spectrum[strip:]
            cosine = factor[0, :, lanes]
            sine = factor[1, :, lanes] * hand(u)
            turned[u, 0:strip, lanes] = (re * cosine - im * sine).astype(BF16)
            turned[u, strip:, lanes] = (im * cosine + re * sine).astype(BF16)
            return carry

        lax.fori_loop(0, tiles, product, 0)

        @pl.when(z > 0)
        def _():
            wait_bytes(ptx.at[u, pl.ds(0, bands - 1)], back_send.at[u])

        def back(i, carry):
            t = lax.rem(b // per_tile + 1 + i, tiles)
            lanes = pl.ds(pl.multiple_of(t * tile, tile), tile)
            partial = jnp.dot(turned[u], table[:, lanes], preferred_element_type=F32).astype(BF16)
            for p in range(per_tile):
                j = t * per_tile + p
                cols = slice(p * strip, (p + 1) * strip)
                ptx[u, j, :, 0:strip] = partial[0:strip, cols]
                ptx[u, j, :, strip:] = partial[strip:, cols]
                src = ptx.at[u, j]
                dst = prx.at[u, pl.ds(pl.multiple_of(b * strip, strip), strip)]

                @pl.when(j != b)
                def _():
                    pltpu.make_async_remote_copy(
                        src,
                        dst,
                        back_send.at[u],
                        back_recv.at[u],
                        device_id={"band": j},
                        device_id_type=MESH,
                    ).start()

                @pl.when(j == b)
                def _():
                    pltpu.make_async_copy(src, dst, back_recv.at[u]).start()

            return carry

        lax.fori_loop(0, tiles, back, 0)

    def to_fields(u):
        wait_bytes(prx.at[u], back_recv.at[u])

        def product(i, carry):
            block = pl.ds(pl.multiple_of(i * tile, tile), tile)
            fields[u, block] = jnp.dot(table[block, :], prx[u], preferred_element_type=F32)
            return carry

        lax.fori_loop(0, tiles, product, 0)

    normalizer = 1.0 / math.sqrt(freqs)

    def send_image(z):
        def term(i, carry):
            block = pl.ds(pl.multiple_of(i * strip, strip), strip)
            value = fields[0, block] * fields[1, block]
            value = (value[:, 0:strip] + value[:, strip:]) * normalizer
            image_tx[z, block] = value.astype(BF16)
            return carry

        lax.fori_loop(0, bands, term, 0)

        def send(d, carry):
            g = lax.rem(f + d, freqs)
            pltpu.make_async_remote_copy(
                image_tx.at[z, pl.ds(pl.multiple_of(g * rows, rows), rows)],
                image_rx.at[z, f],
                image_send.at[z],
                image_recv.at[z],
                device_id={"freq": g},
                device_id_type=MESH,
            ).start()
            return carry

        lax.fori_loop(1, freqs, send, 0)
        pltpu.make_async_copy(
            image_tx.at[z, pl.ds(pl.multiple_of(f * rows, rows), rows)],
            image_rx.at[z, f],
            image_recv.at[z],
        ).start()

    def layer(z, carry):
        for u in range(2):

            @pl.when(z > 0)
            def _():
                to_fields(u)

            to_wavenumbers(z, u)

        @pl.when(z > 0)
        def _():
            send_image(z - 1)

        @pl.when(z == 0)
        def _():
            wait_bytes(slow.at[pl.ds(1, depth - 1)], slow_recv.at[1])
            for later in range(1, depth):
                make_trig(later)

        for u in range(2):
            turn(z, u)
        return carry

    lax.fori_loop(0, depth, layer, 0)
    for u in range(2):
        to_fields(u)
    send_image(depth - 1)
    for u in range(2):
        for c in range(2):
            bottom[0, 2 * u + c] = fields[u, :, c * strip : (c + 1) * strip]

    for z in range(depth):
        wait_bytes(image_rx.at[z], image_recv.at[z])
        image[z] = jnp.sum(image_rx[z].astype(F32), axis=0)

    wait_bytes(chunk_tx.at[pl.ds(0, freqs - 1)], chunk_send)
    wait_bytes(slow.at[0, pl.ds(0, freqs - 1)], slow_send.at[0])
    wait_bytes(slow.at[pl.ds(1, depth - 1), pl.ds(0, freqs - 1)], slow_send.at[1])
    for u in range(2):
        wait_bytes(tx.at[u, :, pl.ds(0, lateral - strip)], fwd_send.at[u])
        wait_bytes(ptx.at[u, pl.ds(0, bands - 1)], back_send.at[u])
    for z in range(depth):
        wait_bytes(image_tx.at[z, pl.ds(0, lateral - rows)], image_send.at[z])


def body(wavefields, slowness_store, owner_plan, freq_slot):
    freqs = lax.axis_size("freq")
    bands = lax.axis_size("band")
    lateral = wavefields.shape[2]
    depth = owner_plan.shape[0]
    strip = lateral // bands
    rows = lateral // freqs
    dims = (freqs, bands, lateral, depth)
    smem = pl.BlockSpec(memory_space=pltpu.SMEM)
    vmem = pl.BlockSpec(memory_space=pltpu.VMEM)
    dma = pltpu.SemaphoreType.DMA
    return pl.pallas_call(
        functools.partial(kernel, dims),
        out_shape=(
            jax.ShapeDtypeStruct((depth, rows, strip), F32),
            jax.ShapeDtypeStruct((1, 4, lateral, strip), F32),
        ),
        in_specs=[smem, smem, vmem, vmem, pl.BlockSpec(memory_space=pl.ANY)],
        out_specs=(vmem, vmem),
        scratch_shapes=[
            pltpu.VMEM((2, lateral, 2 * strip), F32),
            pltpu.VMEM((2, lateral, 2 * strip), BF16),
            pltpu.VMEM((2, 2, lateral, strip), BF16),
            pltpu.VMEM((2, 2, strip, lateral), BF16),
            pltpu.VMEM((2, 2 * strip, lateral), BF16),
            pltpu.VMEM((2, bands, strip, 2 * strip), BF16),
            pltpu.VMEM((2, lateral, 2 * strip), BF16),
            pltpu.VMEM((depth, 2, lateral, strip), F32),
            pltpu.VMEM((2, strip, lateral), F32),
            pltpu.VMEM((freqs, rows + 16, strip), BF16),
            pltpu.VMEM((freqs, rows + 16, strip), BF16),
            pltpu.VMEM((depth, rows, strip), BF16),
            pltpu.VMEM((depth, freqs, rows, strip), BF16),
            pltpu.VMEM((depth, lateral, strip), BF16),
            pltpu.VMEM((depth, freqs, rows, strip), BF16),
            dma,
            dma,
            dma,
            dma((2,)),
            dma((2,)),
            dma((2,)),
            dma((2,)),
            dma((2,)),
            dma((2,)),
            dma((depth,)),
            dma((depth,)),
        ],
        compiler_params=pltpu.CompilerParams(
            collective_id=0, has_side_effects=True, vmem_limit_bytes=48 * 2**20
        ),
    )(owner_plan, freq_slot, jnp.asarray(sine_table(lateral)), slowness_store, wavefields)


def solution(mesh):
    in_specs = (P("freq", None, None, "band"), P("freq", None, "band"), P(), P("freq"))
    out_specs = (P(None, "freq", "band"), P("freq", None, None, "band"))
    return jax.shard_map(body, mesh=mesh, in_specs=in_specs, out_specs=out_specs, check_vma=False)
```

time: 1230 us -> 200 us (0.16)
  waiting for transfers between devices: 809 us -> 0 us
  matrix products: 204 us -> 0 us
  Pallas kernels: 0 us -> 190 us
  blocking collectives: 127 us -> 0 us
  local copies, waits for them, and re-layouts: 28.6 us -> 5.22 us
  other arithmetic: 18.8 us -> 0 us
  between operations: 16.9 us -> 1.3 us
    unnamed x7 -> x0, waiting for transfers between devices: 440 us -> none
    psum x1 -> x0, waiting for transfers between devices: 313 us -> none  [from_root(): return lax.psum(block, axis)]
    dot_general x12 -> x0, matrix products: 204 us -> none  [the longest x3 51.3 us: body(): jnp.einsum('cky,ly->ckl', line_spectrum, band_table, preferred_element_ty...]
    pallas_call x0 -> x1, Pallas kernels: none -> 190 us  [body(): pl.pallas_call(functools.partial(kernel, dims), out_shape=(jax.ShapeDtype...]
    all_to_all x4 -> x0, blocking collectives: 127 us -> none  [the longest x2 63.4 us: body(): lax.all_to_all(half_spectrum, 'band', split_axis=1, concat_axis=2, tiled=...]
    all_to_all x2 -> x0, waiting for transfers between devices: 56 us -> none  [the longest x1 28.8 us: body(): lax.all_to_all(half_spectrum, 'band', split_axis=1, concat_axis=2, tiled=...]
    another operation x7 -> x0, other arithmetic: 17.3 us -> none
  transfers between devices with their start and end apart: 6 -> 0, of which waited for: 6 -> 0; matrix products, arithmetic and copies ran while one was open for 2% -> 0% of each run, Pallas kernels for 0% -> 0%
where the time goes in v1:
time: 200 us; the launch traced here: 197 us
  Pallas kernels  190 us (95%)
  local copies, waits for them, and re-layouts  5.22 us (3%)
    pallas_call x1, Pallas kernels, body(): pl.pallas_call(functools.partial(kernel, dims), out_shape=(jax.ShapeDtype...  190 us
    unnamed x8, local copies, waits for them, and re-layouts  5.22 us

profile of v1, /device:TPU:32, one launch (start us, length us, event | category | flops | bytes accessed | tf_op | source)
XLA Modules:
  0.0 196.8 jit_solution(16990849378785998955)
XLA Ops:
  1.3 0.0 copy-start
  1.3 1.6 copy-done
  2.9 0.0 copy-start.1
  2.9 1.0 copy-done.1
  3.9 0.0 copy-start.2
  3.9 0.7 copy-done.2
  4.6 190.3 %shard_map.68 = (f32[3,32,128]{2,1,0:T(8,128)S(1)}, f32[1,4,1024,128]{3,2,1,0:T(8,128)S(1)}) custom-call(s32[3]{0:T(128)S(1)} %copy-done.2, s32[1]{0:T(128)S(6)} %copy.9.slot, bf16[1024,1024]{1,0:T(8,128)(2,1)S(1)} %copy-done, f32[1,1024,128]{2,1,0:T(8,128)S(1)} %copy-done.1, f32[1,4,1024,128]{3,2,1,0:T(8,128)} %wave.1), custom_call_target="tpu_custom_call" | custom-call | tf_op jit(solution)/shard_map/pallas_call | solution.py:380
  194.9 0.6 copy.10
  195.5 1.3 copy.11
Async XLA Ops:
  1.3 1.6 copy-start
  2.9 1.0 copy-start.1
  3.9 0.7 copy-start.2

commit v2 on v1

v2 whole, which is shorter than its diff:
```python
import functools
import math

import jax
import jax.numpy as jnp
import numpy as np
from jax import lax
from jax.experimental import pallas as pl
from jax.experimental.pallas import tpu as pltpu
from jax.sharding import PartitionSpec as P

OMEGA_LO = 1.5
OMEGA_HI = 3.0
MESH = pl.DeviceIdType.MESH
BF16 = jnp.bfloat16
F32 = jnp.float32


def sine_table(length):
    ordinal = np.arange(1, length + 1, dtype=np.int64)
    modulo = ordinal[:, None] * ordinal[None, :] % (2 * (length + 1))
    angles = math.pi * modulo / (length + 1)
    return (math.sqrt(2.0 / (length + 1)) * np.sin(angles)).astype(np.float32).astype(BF16)


def small_cos_sin(phi):
    p2 = phi * phi
    cosine = 1.0 + p2 * (-1 / 2 + p2 * (1 / 24 + p2 * (-1 / 720 + p2 * (1 / 40320))))
    sine = phi * (1.0 + p2 * (-1 / 6 + p2 * (1 / 120 + p2 * (-1 / 5040 + p2 * (1 / 362880)))))
    return cosine, sine


def kernel(
    dims,
    owner,
    slot,
    table,
    slab,
    wave,
    image,
    bottom,
    fields,
    shifted,
    tx,
    mid,
    rx,
    turned,
    ptx,
    prx,
    last,
    trig,
    factor,
    chunk_tx,
    chunk_rx,
    select,
    slow,
    column,
    slow_mid,
    cross_tx,
    cross_rx,
    plane_tx,
    plane_rx,
    column_tx,
    column_rx,
    image_tx,
    image_rx,
    load_sem,
    chunk_send,
    chunk_recv,
    slow_send,
    slow_recv,
    column_send,
    column_recv,
    slow_mid_send,
    slow_mid_recv,
    fwd_send,
    fwd_recv,
    mid_send,
    mid_recv,
    back_send,
    back_recv,
    last_send,
    last_recv,
    cross_send,
    cross_recv,
    plane_send,
    plane_recv,
    up_send,
    up_recv,
    image_send,
    image_recv,
):
    freqs, bands, lateral, depth = dims
    n = bands // 2
    strip = lateral // bands
    rows = lateral // freqs
    tile = 2 * strip
    f = lax.axis_index("freq")
    b = lax.axis_index("band")
    x, y, l = lax.rem(f, n), lax.rem(f // n, n), f // (n * n)
    h, c = b // 2, lax.rem(b, 2)
    z = 2 * h + l
    ring = (x, y)
    other = (y, x)
    home = tuple(lax.rem(h - other[u] + n, n) for u in range(2))
    numbers = (l * n * n + y * n + home[0], l * n * n + home[1] * n + x)
    strips = tuple(2 * ring[u] + c for u in range(2))

    def at(u, r, o, zz, cc):
        xx, yy = (r, o) if u == 0 else (o, r)
        return {"freq": (lax.rem(zz, 2) * n + yy) * n + xx, "band": (zz // 2) * 2 + cc}

    def wait_bytes(ref, sem):
        pltpu.make_async_copy(ref, ref, sem).wait()

    def remote(src, dst, send_sem, recv_sem, target):
        pltpu.make_async_remote_copy(
            src, dst, send_sem, recv_sem, device_id=target, device_id_type=MESH
        ).start()

    def send(src, dst, send_sem, recv_sem, target, here):
        @pl.when(jnp.logical_not(here))
        def _():
            remote(src, dst, send_sem, recv_sem, target)

        @pl.when(here)
        def _():
            pltpu.make_async_copy(src, dst, recv_sem).start()

    def loop(first, count, body):
        def step(i, carry):
            body(i)
            return carry

        lax.fori_loop(first, count, step, 0)

    def aligned(i, size):
        return pl.ds(pl.multiple_of(i * size, size), size)

    barrier = pltpu.get_barrier_semaphore()

    def greet(axis, me, count):
        def body(d):
            pl.semaphore_signal(
                barrier, inc=1, device_id={axis: lax.rem(me + d, count)}, device_id_type=MESH
            )

        loop(1, count, body)

    greet("freq", f, freqs)
    greet("band", b, bands)
    loads = [
        pltpu.make_async_copy(
            wave.at[0, 2 * u + k], fields.at[u, :, pl.ds(k * strip, strip)], load_sem
        )
        for u in range(2)
        for k in range(2)
    ]
    for load in loads:
        load.start()
    chunk_tx[:, 0:rows, :] = (slab[0] - 1.0).astype(BF16).reshape(freqs, rows, strip)
    chunk_tx[:, rows:, :] = jnp.full((freqs, 16, strip), slot[0].astype(F32)).astype(BF16)
    pl.semaphore_wait(barrier, freqs + bands - 2)

    def send_chunk(d):
        g = lax.rem(f + d, freqs)
        remote(chunk_tx.at[g], chunk_rx.at[f], chunk_send, chunk_recv, {"freq": g})

    loop(1, freqs, send_chunk)
    pltpu.make_async_copy(chunk_tx.at[f], chunk_rx.at[f], chunk_recv).start()

    def omega_of(number):
        return OMEGA_LO + (OMEGA_HI - OMEGA_LO) * (number.astype(F32) + 0.5) / freqs

    omega = omega_of(slot[0])

    wait_bytes(chunk_rx, chunk_recv)
    for k in range(depth):
        select[k] = chunk_rx[owner[k], 0:rows, :]

    def send_slow(d):
        g = lax.rem(f + d, freqs)
        remote(select.at[0], slow.at[f], slow_send, slow_recv, {"freq": g})

    loop(1, freqs, send_slow)
    pltpu.make_async_copy(select.at[0], slow.at[f], slow_recv).start()

    def send_column(d):
        zz = lax.rem(z + d, bands)
        remote(
            select.at[pl.ds(1, depth - 1)],
            column.at[z],
            column_send,
            column_recv,
            at(0, x, y, zz, c),
        )

    loop(1, bands, send_column)
    pltpu.make_async_copy(select.at[pl.ds(1, depth - 1)], column.at[z], column_recv).start()

    def send_planes():
        wait_bytes(column, column_recv)
        for u in range(2):

            def body(i, u=u):
                hh, oo = i // n, lax.rem(i, n)
                send(
                    column.at[pl.ds(2 * hh, 2)],
                    slow_mid.at[u, :, y * n + x],
                    slow_mid_send.at[u],
                    slow_mid_recv.at[u],
                    at(u, hh, oo, z, c),
                    (hh == ring[u]) & (oo == other[u]),
                )

            loop(0, n * n, body)

    def make_factor(u):
        mine = omega_of(chunk_rx[numbers[u], rows : rows + 16, :])[0:1]

        def body(i):
            shape = (strip, strip)
            kx = (lax.broadcasted_iota(jnp.int32, shape, 0) + (strips[u] * strip + 1)).astype(F32)
            ky = (lax.broadcasted_iota(jnp.int32, shape, 1) + (i * strip + 1)).astype(F32)
            kx = math.pi * kx / (lateral + 1)
            ky = math.pi * ky / (lateral + 1)
            q = mine * mine - kx * kx - ky * ky
            theta = jnp.sqrt(jnp.maximum(q, 0.0))
            damp = jnp.exp(-jnp.sqrt(jnp.maximum(-q, 0.0)))
            factor[u, 0, :, aligned(i, strip)] = damp * jnp.cos(theta)
            factor[u, 1, :, aligned(i, strip)] = damp * jnp.sin(theta)

        loop(0, bands, body)

    def make_first_trig():
        def body(g):
            cosine, sine = small_cos_sin(omega * slow[g].astype(F32))
            trig[0, 0, aligned(g, rows)] = cosine
            trig[0, 1, aligned(g, rows)] = sine

        loop(0, freqs, body)

    def make_trig(step, u):
        mine = omega_of(chunk_rx[numbers[u], rows : rows + 16, :])[0:1]

        def body(g):
            value = slow_mid[u, g // (n * n), lax.rem(g, n * n), step - 1]
            cosine, sine = small_cos_sin(mine * value.astype(F32))
            trig[2 * step - 1 + u, 0, aligned(g, rows)] = cosine
            trig[2 * step - 1 + u, 1, aligned(g, rows)] = sine

        loop(0, freqs, body)

    def hand(u):
        return -1.0 if u == 0 else 1.0

    def to_wavenumbers(step, u):
        phase = 0 if step == 0 else 2 * step - 1 + u

        def shift(i):
            block = aligned(i, strip)
            cosine = trig[phase, 0, block]
            sine = trig[phase, 1, block] * hand(u)
            re = fields[u, block, 0:strip]
            im = fields[u, block, strip:]
            shifted[u, block, 0:strip] = (re * cosine - im * sine).astype(BF16)
            shifted[u, block, strip:] = (im * cosine + re * sine).astype(BF16)

        loop(0, bands, shift)
        if step > 0:
            wait_bytes(tx.at[u, :, pl.ds(0, lateral - strip)], fwd_send.at[u])

        def product(i):
            t = lax.rem(ring[u] + 1 + i, n)
            block = aligned(t, tile)
            half = jnp.dot(table[block, :], shifted[u], preferred_element_type=F32).astype(BF16)
            tx[u, 0, block] = half[:, 0:strip]
            tx[u, 1, block] = half[:, strip:]
            for p in range(2):
                j = 2 * t + p
                if step == 0:
                    dst = mid.at[u, ring[u], :, :, aligned(c, strip)]
                    sem = mid_recv.at[u, ring[u]]
                else:
                    dst = rx.at[u, :, :, aligned(strips[u], strip)]
                    sem = fwd_recv.at[u]
                send(
                    tx.at[u, :, aligned(j, strip)],
                    dst,
                    fwd_send.at[u],
                    sem,
                    at(u, t, other[u], z, p),
                    j == strips[u],
                )

        loop(0, n, product)

    def forward(u):
        def body(i):
            q = lax.rem(ring[u] + i, n)
            wait_bytes(mid.at[u, q], mid_recv.at[u, q])
            hh = lax.rem(q + other[u], n)
            send(
                mid.at[u, q],
                rx.at[u, :, :, aligned(h, tile)],
                mid_send.at[u],
                fwd_recv.at[u],
                at(u, ring[u], other[u], 2 * hh + l, c),
                hh == h,
            )

        loop(0, n, body)

    def turn(step, u):
        wait_bytes(rx.at[u], fwd_recv.at[u])

        def product(i):
            lanes = aligned(i, tile)
            lines = rx[u].reshape(2 * strip, lateral)
            spectrum = jnp.dot(lines, table[:, lanes], preferred_element_type=F32)
            re = spectrum[0:strip]
            im = spectrum[strip:]
            cosine = factor[u, 0, :, lanes]
            sine = factor[u, 1, :, lanes] * hand(u)
            turned[u, 0:strip, lanes] = (re * cosine - im * sine).astype(BF16)
            turned[u, strip:, lanes] = (im * cosine + re * sine).astype(BF16)

        loop(0, n, product)
        if step > 0:
            wait_bytes(ptx.at[u, pl.ds(0, bands - 1)], back_send.at[u])
        final = step == depth - 1

        def back(i):
            t = lax.rem((h if final else ring[u]) + 1 + i, n)
            lanes = aligned(t, tile)
            partial = jnp.dot(turned[u], table[:, lanes], preferred_element_type=F32).astype(BF16)
            for p in range(2):
                j = 2 * t + p
                cols = slice(p * strip, (p + 1) * strip)
                ptx[u, j, :, 0:strip] = partial[0:strip, cols]
                ptx[u, j, :, strip:] = partial[strip:, cols]
                block = aligned(strips[u], strip)
                if final:
                    send(
                        ptx.at[u, j],
                        last.at[u, block],
                        last_send.at[u],
                        last_recv.at[u],
                        at(u, home[u], other[u], 2 * t + l, p),
                        (home[u] == ring[u]) & (j == b),
                    )
                else:
                    send(
                        ptx.at[u, j],
                        prx.at[u, block],
                        back_send.at[u],
                        back_recv.at[u],
                        at(u, t, other[u], z, p),
                        j == strips[u],
                    )

        loop(0, n, back)

    def to_fields(u, source, sem):
        wait_bytes(source.at[u], sem.at[u])

        def product(i):
            block = aligned(i, tile)
            fields[u, block] = jnp.dot(table[block, :], source[u], preferred_element_type=F32)

        loop(0, n, product)

    normalizer = 1.0 / math.sqrt(freqs)

    def send_cross(step):
        def body(i):
            cross_tx[step, aligned(i, strip)] = fields[1, aligned(i, strip)].astype(BF16)

        loop(0, bands, body)
        send(
            cross_tx.at[step],
            cross_rx.at[step],
            cross_send.at[step],
            cross_recv.at[step],
            at(0, y, home[1], z, c),
            (x == y) & (home[1] == y),
        )

    def send_terms(step):
        wait_bytes(cross_rx.at[step], cross_recv.at[step])

        def body(g):
            block = aligned(g, rows)
            value = fields[0, block] * cross_rx[step, block].astype(F32)
            value = (value[:, 0:strip] + value[:, strip:]) * normalizer
            plane_tx[step, g // (n * n), lax.rem(g, n * n)] = value.astype(BF16)

        loop(0, freqs, body)

        def body_send(i):
            g = lax.rem(y * n + x + i, n * n)
            send(
                plane_tx.at[step, :, g],
                plane_rx.at[step, x, y],
                plane_send.at[step],
                plane_recv.at[step],
                at(0, lax.rem(g, n), g // n, z, c),
                i == 0,
            )

        loop(0, n * n, body_send)

    def send_sums(step):
        wait_bytes(plane_rx.at[step], plane_recv.at[step])

        def body(i):
            zz = lax.rem(z + i, bands)
            total = jnp.zeros((rows, strip), F32)
            for yy in range(n):
                total += plane_rx[step, zz // 2, yy, lax.rem(zz, 2)].astype(F32)
            column_tx[step, zz] = total.astype(BF16)
            send(
                column_tx.at[step, zz],
                column_rx.at[step, z],
                up_send.at[step],
                up_recv.at[step],
                at(0, x, y, zz, c),
                i == 0,
            )

        loop(0, bands, body)

    def send_image():
        def term(i):
            block = aligned(i, strip)
            value = fields[0, block] * fields[1, block]
            value = (value[:, 0:strip] + value[:, strip:]) * normalizer
            image_tx[block] = value.astype(BF16)

        loop(0, bands, term)

        def body(d):
            g = lax.rem(f + d, freqs)
            remote(
                image_tx.at[aligned(g, rows)], image_rx.at[f], image_send, image_recv, {"freq": g}
            )

        loop(1, freqs, body)
        pltpu.make_async_copy(image_tx.at[aligned(f, rows)], image_rx.at[f], image_recv).start()

    for load in loads:
        load.wait()
    wait_bytes(slow, slow_recv)
    make_first_trig()
    for step in range(depth):
        for u in range(2):
            if step > 0:
                to_fields(u, prx, back_recv)
            to_wavenumbers(step, u)
        if step == 0:
            for u in range(2):
                forward(u)
            send_planes()
            for u in range(2):
                make_factor(u)
        else:
            send_cross(step - 1)
        for u in range(2):
            turn(step, u)
        if step > 0:
            send_terms(step - 1)
        if step == 0:
            for u in range(2):
                wait_bytes(slow_mid.at[u], slow_mid_recv.at[u])
        if step < depth - 1:
            for u in range(2):
                make_trig(step + 1, u)
        if step > 1:
            send_sums(step - 2)
    send_sums(depth - 2)
    for u in range(2):
        to_fields(u, last, last_recv)
    send_image()
    for u in range(2):
        for k in range(2):
            bottom[0, 2 * u + k] = fields[u, :, k * strip : (k + 1) * strip]

    for step in range(depth - 1):
        wait_bytes(column_rx.at[step], up_recv.at[step])
        image[step] = jnp.sum(column_rx[step].astype(F32), axis=0)
    wait_bytes(image_rx, image_recv)
    image[depth - 1] = jnp.sum(image_rx[...].astype(F32), axis=0)

    wait_bytes(chunk_tx.at[pl.ds(0, freqs - 1)], chunk_send)
    wait_bytes(slow.at[pl.ds(0, freqs - 1)], slow_send)
    wait_bytes(column.at[pl.ds(0, bands - 1)], column_send)
    for u in range(2):
        wait_bytes(slow_mid.at[u, :, pl.ds(0, n * n - 1)], slow_mid_send.at[u])
        wait_bytes(mid.at[u, pl.ds(0, n - 1)], mid_send.at[u])
        wait_bytes(tx.at[u, :, pl.ds(0, lateral - strip)], fwd_send.at[u])
        wait_bytes(ptx.at[u, pl.ds(0, bands - 1)], last_send.at[u])

        @pl.when(home[u] != ring[u])
        def _():
            wait_bytes(ptx.at[u, 0], last_send.at[u])

    for step in range(depth - 1):

        @pl.when(jnp.logical_not((x == y) & (home[1] == y)))
        def _():
            wait_bytes(cross_tx.at[step], cross_send.at[step])

        wait_bytes(plane_tx.at[step, :, pl.ds(0, n * n - 1)], plane_send.at[step])
        wait_bytes(column_tx.at[step, pl.ds(0, bands - 1)], up_send.at[step])
    wait_bytes(image_tx.at[pl.ds(0, lateral - rows)], image_send)


def body(wavefields, slowness_store, owner_plan, freq_slot):
    freqs = lax.axis_size("freq")
    bands = lax.axis_size("band")
    lateral = wavefields.shape[2]
    depth = owner_plan.shape[0]
    n = bands // 2
    strip = lateral // bands
    rows = lateral // freqs
    dims = (freqs, bands, lateral, depth)
    smem = pl.BlockSpec(memory_space=pltpu.SMEM)
    vmem = pl.BlockSpec(memory_space=pltpu.VMEM)
    dma = pltpu.SemaphoreType.DMA
    return pl.pallas_call(
        functools.partial(kernel, dims),
        out_shape=(
            jax.ShapeDtypeStruct((depth, rows, strip), F32),
            jax.ShapeDtypeStruct((1, 4, lateral, strip), F32),
        ),
        in_specs=[smem, smem, vmem, vmem, pl.BlockSpec(memory_space=pl.ANY)],
        out_specs=(vmem, vmem),
        scratch_shapes=[
            pltpu.VMEM((2, lateral, 2 * strip), F32),
            pltpu.VMEM((2, lateral, 2 * strip), BF16),
            pltpu.VMEM((2, 2, lateral, strip), BF16),
            pltpu.VMEM((2, n, 2, strip, 2 * strip), BF16),
            pltpu.VMEM((2, 2, strip, lateral), BF16),
            pltpu.VMEM((2, 2 * strip, lateral), BF16),
            pltpu.VMEM((2, bands, strip, 2 * strip), BF16),
            pltpu.VMEM((2, lateral, 2 * strip), BF16),
            pltpu.VMEM((2, lateral, 2 * strip), BF16),
            pltpu.VMEM((2 * depth - 1, 2, lateral, strip), F32),
            pltpu.VMEM((2, 2, strip, lateral), F32),
            pltpu.VMEM((freqs, rows + 16, strip), BF16),
            pltpu.VMEM((freqs, rows + 16, strip), BF16),
            pltpu.VMEM((depth, rows, strip), BF16),
            pltpu.VMEM((freqs, rows, strip), BF16),
            pltpu.VMEM((bands, depth - 1, rows, strip), BF16),
            pltpu.VMEM((2, 2, n * n, depth - 1, rows, strip), BF16),
            pltpu.VMEM((depth - 1, lateral, 2 * strip), BF16),
            pltpu.VMEM((depth - 1, lateral, 2 * strip), BF16),
            pltpu.VMEM((depth - 1, 2, n * n, rows, strip), BF16),
            pltpu.VMEM((depth - 1, n, n, 2, rows, strip), BF16),
            pltpu.VMEM((depth - 1, bands, rows, strip), BF16),
            pltpu.VMEM((depth - 1, bands, rows, strip), BF16),
            pltpu.VMEM((lateral, strip), BF16),
            pltpu.VMEM((freqs, rows, strip), BF16),
            dma,
            dma,
            dma,
            dma,
            dma,
            dma,
            dma,
            dma((2,)),
            dma((2,)),
            dma((2,)),
            dma((2,)),
            dma((2,)),
            dma((2, n)),
            dma((2,)),
            dma((2,)),
            dma((2,)),
            dma((2,)),
            dma((depth - 1,)),
            dma((depth - 1,)),
            dma((depth - 1,)),
            dma((depth - 1,)),
            dma((depth - 1,)),
            dma((depth - 1,)),
            dma,
            dma,
        ],
        compiler_params=pltpu.CompilerParams(
            collective_id=0, has_side_effects=True, vmem_limit_bytes=52 * 2**20
        ),
    )(owner_plan, freq_slot, jnp.asarray(sine_table(lateral)), slowness_store, wavefields)


def solution(mesh):
    in_specs = (P("freq", None, None, "band"), P("freq", None, "band"), P(), P("freq"))
    out_specs = (P(None, "freq", "band"), P("freq", None, None, "band"))
    return jax.shard_map(body, mesh=mesh, in_specs=in_specs, out_specs=out_specs, check_vma=False)
```

time: 200 us -> 178 us (0.89)
  Pallas kernels: 190 us -> 168 us
    pallas_call x1, Pallas kernels: 190 us -> 168 us  [body(): pl.pallas_call(functools.partial(kernel, dims), out_shape=(jax.ShapeDtype...]
    unnamed x8 -> x6, local copies, waits for them, and re-layouts: 5.22 us -> 5.36 us
where the time goes in v2:
time: 178 us; the launch traced here: 175 us
  Pallas kernels  168 us (94%)
  local copies, waits for them, and re-layouts  5.36 us (3%)
    pallas_call x1, Pallas kernels, body(): pl.pallas_call(functools.partial(kernel, dims), out_shape=(jax.ShapeDtype...  168 us
    unnamed x6, local copies, waits for them, and re-layouts  5.36 us

profile of v2, /device:TPU:32, one launch (start us, length us, event | category | flops | bytes accessed | tf_op | source)
XLA Modules:
  0.0 174.9 jit_solution(10069685019220244151)
XLA Ops:
  1.3 0.0 copy-start
  1.3 1.0 copy-done
  2.3 0.0 copy-start.1
  2.3 0.7 copy-done.1
  3.0 168.2 %shard_map.68 = (f32[3,32,128]{2,1,0:T(8,128)S(1)}, f32[1,4,1024,128]{3,2,1,0:T(8,128)}) custom-call(s32[3]{0:T(128)S(1)} %copy-done.1, s32[1]{0:T(128)S(6)} %copy.9.slot, bf16[1024,1024]{1,0:T(8,128)(2,1)} %constant.2.clone.table, f32[1,1024,128]{2,1,0:T(8,128)S(1)} %copy-done, f32[1,4,1024,128]{3,2,1,0:T(8,128)} %wave.1), custom_call_target="tpu_custom_call" | custom-call | tf_op jit(solution)/shard_map/pallas_call | solution.py:530
  171.2 0.6 copy.10
  171.8 3.0 %copy.11 = f32[1,4,1024,128]{3,2,1,0:T(8,128)} copy(f32[1,4,1024,128]{3,2,1,0:T(8,128)} %get-tuple-element.5) | data formatting | bytes 4194304
Async XLA Ops:
  1.3 1.0 copy-start
  2.3 0.7 copy-start.1

commit v3 on v2

--- a/solution.py
+++ b/solution.py
@@ -56,6 +56,7 @@
     slow,
     column,
     slow_mid,
+    keep,
     cross_tx,
     cross_rx,
     plane_tx,
@@ -104,7 +105,11 @@
     other = (y, x)
     home = tuple(lax.rem(h - other[u] + n, n) for u in range(2))
     numbers = (l * n * n + y * n + home[0], l * n * n + home[1] * n + x)
-    strips = tuple(2 * ring[u] + c for u in range(2))
+    place = (x, lax.rem(y - x + n, n))
+    strips = tuple(2 * place[u] + c for u in range(2))
+
+    def spot(u, t, o):
+        return t if u == 0 else lax.rem(t + o, n)
 
     def at(u, r, o, zz, cc):
         xx, yy = (r, o) if u == 0 else (o, r)
@@ -209,8 +214,8 @@
                     slow_mid.at[u, :, y * n + x],
                     slow_mid_send.at[u],
                     slow_mid_recv.at[u],
-                    at(u, hh, oo, z, c),
-                    (hh == ring[u]) & (oo == other[u]),
+                    at(u, spot(u, hh, oo), oo, z, c),
+                    (hh == place[u]) & (oo == other[u]),
                 )
 
             loop(0, n * n, body)
@@ -271,7 +276,7 @@
             wait_bytes(tx.at[u, :, pl.ds(0, lateral - strip)], fwd_send.at[u])
 
         def product(i):
-            t = lax.rem(ring[u] + 1 + i, n)
+            t = lax.rem(place[u] + 1 + i, n)
             block = aligned(t, tile)
             half = jnp.dot(table[block, :], shifted[u], preferred_element_type=F32).astype(BF16)
             tx[u, 0, block] = half[:, 0:strip]
@@ -289,7 +294,7 @@
                     dst,
                     fwd_send.at[u],
                     sem,
-                    at(u, t, other[u], z, p),
+                    at(u, spot(u, t, other[u]), other[u], z, p),
                     j == strips[u],
                 )
 
@@ -331,7 +336,7 @@
         final = step == depth - 1
 
         def back(i):
-            t = lax.rem((h if final else ring[u]) + 1 + i, n)
+            t = lax.rem((h if final else place[u]) + 1 + i, n)
             lanes = aligned(t, tile)
             partial = jnp.dot(turned[u], table[:, lanes], preferred_element_type=F32).astype(BF16)
             for p in range(2):
@@ -355,7 +360,7 @@
                         prx.at[u, block],
                         back_send.at[u],
                         back_recv.at[u],
-                        at(u, t, other[u], z, p),
+                        at(u, spot(u, t, other[u]), other[u], z, p),
                         j == strips[u],
                     )
 
@@ -372,18 +377,22 @@
 
     normalizer = 1.0 / math.sqrt(freqs)
 
+    def keep_fields(step):
+        def body(i):
+            block = aligned(i, strip)
+            keep[step, block] = fields[0, block].astype(BF16)
+            cross_tx[step, block] = fields[1, block].astype(BF16)
+
+        loop(0, bands, body)
+
     def send_cross(step):
-        def body(i):
-            cross_tx[step, aligned(i, strip)] = fields[1, aligned(i, strip)].astype(BF16)
-
-        loop(0, bands, body)
         send(
             cross_tx.at[step],
             cross_rx.at[step],
             cross_send.at[step],
             cross_recv.at[step],
-            at(0, y, home[1], z, c),
-            (x == y) & (home[1] == y),
+            at(0, place[1], home[1], z, c),
+            (place[1] == x) & (home[1] == y),
         )
 
     def send_terms(step):
@@ -391,7 +400,7 @@
 
         def body(g):
             block = aligned(g, rows)
-            value = fields[0, block] * cross_rx[step, block].astype(F32)
+            value = keep[step, block].astype(F32) * cross_rx[step, block].astype(F32)
             value = (value[:, 0:strip] + value[:, strip:]) * normalizer
             plane_tx[step, g // (n * n), lax.rem(g, n * n)] = value.astype(BF16)
 
@@ -448,6 +457,8 @@
         loop(1, freqs, body)
         pltpu.make_async_copy(image_tx.at[aligned(f, rows)], image_rx.at[f], image_recv).start()
 
+    for u in range(2):
+        make_factor(u)
     for load in loads:
         load.wait()
     wait_bytes(slow, slow_recv)
@@ -461,26 +472,26 @@
             for u in range(2):
                 forward(u)
             send_planes()
-            for u in range(2):
-                make_factor(u)
         else:
-            send_cross(step - 1)
+            keep_fields(step - 1)
         for u in range(2):
             turn(step, u)
         if step > 0:
-            send_terms(step - 1)
+            send_cross(step - 1)
         if step == 0:
             for u in range(2):
                 wait_bytes(slow_mid.at[u], slow_mid_recv.at[u])
         if step < depth - 1:
             for u in range(2):
                 make_trig(step + 1, u)
-        if step > 1:
-            send_sums(step - 2)
-    send_sums(depth - 2)
+    for step in range(depth - 1):
+        send_terms(step)
+    for step in range(depth - 2):
+        send_sums(step)
     for u in range(2):
         to_fields(u, last, last_recv)
     send_image()
+    send_sums(depth - 2)
     for u in range(2):
         for k in range(2):
             bottom[0, 2 * u + k] = fields[u, :, k * strip : (k + 1) * strip]
@@ -506,7 +517,7 @@
 
     for step in range(depth - 1):
 
-        @pl.when(jnp.logical_not((x == y) & (home[1] == y)))
+        @pl.when(jnp.logical_not((place[1] == x) & (home[1] == y)))
         def _():
             wait_bytes(cross_tx.at[step], cross_send.at[step])
 
@@ -555,6 +566,7 @@
             pltpu.VMEM((2, 2, n * n, depth - 1, rows, strip), BF16),
             pltpu.VMEM((depth - 1, lateral, 2 * strip), BF16),
             pltpu.VMEM((depth - 1, lateral, 2 * strip), BF16),
+            pltpu.VMEM((depth - 1, lateral, 2 * strip), BF16),
             pltpu.VMEM((depth - 1, 2, n * n, rows, strip), BF16),
             pltpu.VMEM((depth - 1, n, n, 2, rows, strip), BF16),
             pltpu.VMEM((depth - 1, bands, rows, strip), BF16),
@@ -588,7 +600,7 @@
             dma,
         ],
         compiler_params=pltpu.CompilerParams(
-            collective_id=0, has_side_effects=True, vmem_limit_bytes=52 * 2**20
+            collective_id=0, has_side_effects=True, vmem_limit_bytes=36 * 2**20
         ),
     )(owner_plan, freq_slot, jnp.asarray(sine_table(lateral)), slowness_store, wavefields)
 

time: 178 us -> 154 us (0.87); the launches traced: 175 us -> 154 us
  Pallas kernels: 168 us -> 146 us
    pallas_call x1, Pallas kernels: 168 us -> 146 us  [body(): pl.pallas_call(functools.partial(kernel, dims), out_shape=(jax.ShapeDtype...]
    unnamed x6 -> x10, local copies, waits for them, and re-layouts: 5.36 us -> 6.81 us
where the time goes in v3:
time: 154 us
  Pallas kernels  146 us (95%)
  local copies, waits for them, and re-layouts  6.81 us (4%)
    pallas_call x1, Pallas kernels, body(): pl.pallas_call(functools.partial(kernel, dims), out_shape=(jax.ShapeDtype...  146 us
    unnamed x10, local copies, waits for them, and re-layouts  6.81 us

profile of v3, /device:TPU:32, one launch (start us, length us, event | category | flops | bytes accessed | tf_op | source)
XLA Modules:
  0.0 153.7 jit_solution(13085684782670730256)
XLA Ops:
  1.3 0.0 copy-start
  1.3 1.6 %copy-done = f32[1,4,1024,128]{3,2,1,0:T(8,128)S(1)} copy-done((f32[1,4,1024,128]{3,2,1,0:T(8,128)S(1)}, f32[1,4,1024,128]{3,2,1,0:T(8,128)}, u32[]{:S(2)}) %copy-start) | copy-done | bytes 2097176
  2.9 0.0 copy-start.1
  2.9 1.6 %copy-done.1 = bf16[1024,1024]{1,0:T(8,128)(2,1)S(1)} copy-done((bf16[1024,1024]{1,0:T(8,128)(2,1)S(1)}, bf16[1024,1024]{1,0:T(8,128)(2,1)}, u32[]{:S(2)}) %copy-start.1) | copy-done | bytes 2097176
  4.5 0.0 copy-start.2
  4.5 1.0 copy-done.2
  5.5 0.0 copy-start.3
  5.5 0.7 copy-done.3
  6.2 145.6 %shard_map.68 = (f32[3,32,128]{2,1,0:T(8,128)S(1)}, f32[1,4,1024,128]{3,2,1,0:T(8,128)S(1)}) custom-call(s32[3]{0:T(128)S(1)} %copy-done.3, s32[1]{0:T(128)S(6)} %copy.9.slot, bf16[1024,1024]{1,0:T(8,128)(2,1)S(1)} %copy-done.1, f32[1,1024,128]{2,1,0:T(8,128)S(1)} %copy-done.2, f32[1,4,1024,128]{3,2,1,0:T(8,128)S(1)} %copy-done), custom_call_target="tpu_custom_call" | custom-call | tf_op jit(solution)/shard_map/pallas_call | solution.py:541
  151.7 0.6 copy.10
  152.4 1.3 copy.11
Async XLA Ops:
  1.3 1.6 %copy-start = (f32[1,4,1024,128]{3,2,1,0:T(8,128)S(1)}, f32[1,4,1024,128]{3,2,1,0:T(8,128)}, u32[]{:S(2)}) copy-start(f32[1,4,1024,128]{3,2,1,0:T(8,128)} %wave.1) | copy-start | bytes 6291460
  2.9 1.6 %copy-start.1 = (bf16[1024,1024]{1,0:T(8,128)(2,1)S(1)}, bf16[1024,1024]{1,0:T(8,128)(2,1)}, u32[]{:S(2)}) copy-start(bf16[1024,1024]{1,0:T(8,128)(2,1)} %constant.2.clone.table) | copy-start | bytes 6291460
  4.5 1.0 copy-start.2
  5.5 0.7 copy-start.3

commit v4 on v2

v4 whole, which is shorter than its diff:
```python
import functools
import math

import jax
import jax.numpy as jnp
import numpy as np
from jax import lax
from jax.experimental import pallas as pl
from jax.experimental.pallas import tpu as pltpu
from jax.sharding import PartitionSpec as P

OMEGA_LO = 1.5
OMEGA_HI = 3.0
MESH = pl.DeviceIdType.MESH
BF16 = jnp.bfloat16
F32 = jnp.float32


def sine_table(length):
    ordinal = np.arange(1, length + 1, dtype=np.int64)
    modulo = ordinal[:, None] * ordinal[None, :] % (2 * (length + 1))
    angles = math.pi * modulo / (length + 1)
    return (math.sqrt(2.0 / (length + 1)) * np.sin(angles)).astype(np.float32).astype(BF16)


def small_cos_sin(phi):
    p2 = phi * phi
    cosine = 1.0 + p2 * (-1 / 2 + p2 * (1 / 24 + p2 * (-1 / 720 + p2 * (1 / 40320))))
    sine = phi * (1.0 + p2 * (-1 / 6 + p2 * (1 / 120 + p2 * (-1 / 5040 + p2 * (1 / 362880)))))
    return cosine, sine


def kernel(
    dims,
    owner,
    slot,
    table_hbm,
    slab_hbm,
    wave,
    image,
    bottom,
    table,
    slab,
    fields,
    shifted,
    tx,
    mid,
    rx,
    turned,
    ptx,
    prx,
    last,
    trig,
    factor,
    chunk_tx,
    chunk_rx,
    select,
    slow,
    column,
    slow_mid,
    kept,
    plane_tx,
    plane_rx,
    column_tx,
    column_rx,
    image_tx,
    image_rx,
    table_sem,
    slab_sem,
    load_sem,
    chunk_send,
    chunk_recv,
    slow_send,
    slow_recv,
    column_send,
    column_recv,
    slow_mid_send,
    slow_mid_recv,
    fwd_send,
    fwd_recv,
    mid_send,
    mid_recv,
    back_send,
    back_recv,
    last_send,
    last_recv,
    plane_send,
    plane_recv,
    up_send,
    up_recv,
    image_send,
    image_recv,
):
    freqs, bands, lateral, depth = dims
    n = bands // 2
    strip = lateral // bands
    rows = lateral // freqs
    tile = 2 * strip
    f = lax.axis_index("freq")
    b = lax.axis_index("band")
    x, y, l = lax.rem(f, n), lax.rem(f // n, n), f // (n * n)
    h, c = b // 2, lax.rem(b, 2)
    z = 2 * h + l
    home = lax.rem(h - y + n, n)
    number = l * n * n + y * n + home
    mine = 2 * x + c

    def at(xx, yy, zz, cc):
        return {"freq": (lax.rem(zz, 2) * n + yy) * n + xx, "band": (zz // 2) * 2 + cc}

    def wait_bytes(ref, sem):
        pltpu.make_async_copy(ref, ref, sem).wait()

    def remote(src, dst, send_sem, recv_sem, target):
        pltpu.make_async_remote_copy(
            src, dst, send_sem, recv_sem, device_id=target, device_id_type=MESH
        ).start()

    def send(src, dst, send_sem, recv_sem, target, here):
        @pl.when(jnp.logical_not(here))
        def _():
            remote(src, dst, send_sem, recv_sem, target)

        @pl.when(here)
        def _():
            pltpu.make_async_copy(src, dst, recv_sem).start()

    def loop(first, count, body):
        def step(i, carry):
            body(i)
            return carry

        lax.fori_loop(first, count, step, 0)

    def aligned(i, size):
        return pl.ds(pl.multiple_of(i * size, size), size)

    slab_load = pltpu.make_async_copy(slab_hbm.at[0], slab, slab_sem)
    table_load = pltpu.make_async_copy(table_hbm, table, table_sem)
    slab_load.start()
    barrier = pltpu.get_barrier_semaphore()

    def greet(axis, me, count):
        def body(d):
            pl.semaphore_signal(
                barrier, inc=1, device_id={axis: lax.rem(me + d, count)}, device_id_type=MESH
            )

        loop(1, count, body)

    greet("freq", f, freqs)
    greet("band", b, bands)
    loads = [
        pltpu.make_async_copy(
            wave.at[0, 2 * u + k], fields.at[u, :, pl.ds(k * strip, strip)], load_sem
        )
        for u in range(2)
        for k in range(2)
    ]
    for load in loads:
        load.start()
    table_load.start()
    slab_load.wait()
    chunk_tx[:, 0:rows, :] = (slab[...] - 1.0).astype(BF16).reshape(freqs, rows, strip)
    chunk_tx[:, rows:, :] = jnp.full((freqs, 16, strip), slot[0].astype(F32)).astype(BF16)
    pl.semaphore_wait(barrier, freqs + bands - 2)

    def send_chunk(d):
        g = lax.rem(f + d, freqs)
        remote(chunk_tx.at[g], chunk_rx.at[f], chunk_send, chunk_recv, {"freq": g})

    loop(1, freqs, send_chunk)
    pltpu.make_async_copy(chunk_tx.at[f], chunk_rx.at[f], chunk_recv).start()

    def omega_of(number):
        return OMEGA_LO + (OMEGA_HI - OMEGA_LO) * (number.astype(F32) + 0.5) / freqs

    omega = omega_of(slot[0])

    wait_bytes(chunk_rx, chunk_recv)
    for k in range(depth):
        select[k] = chunk_rx[owner[k], 0:rows, :]

    def send_slow(d):
        g = lax.rem(f + d, freqs)
        remote(select.at[0], slow.at[f], slow_send, slow_recv, {"freq": g})

    loop(1, freqs, send_slow)
    pltpu.make_async_copy(select.at[0], slow.at[f], slow_recv).start()

    def send_column(d):
        zz = lax.rem(z + d, bands)
        remote(
            select.at[pl.ds(1, depth - 1)],
            column.at[z],
            column_send,
            column_recv,
            at(x, y, zz, c),
        )

    loop(1, bands, send_column)
    pltpu.make_async_copy(select.at[pl.ds(1, depth - 1)], column.at[z], column_recv).start()

    def send_planes():
        wait_bytes(column, column_recv)

        def body(i):
            xx, yy = lax.rem(x + i // n, n), lax.rem(y + i, n)
            send(
                column.at[pl.ds(2 * xx, 2)],
                slow_mid.at[:, y * n + x],
                slow_mid_send,
                slow_mid_recv,
                at(xx, yy, z, c),
                i == 0,
            )

        loop(0, n * n, body)

    def omega_here():
        return omega_of(chunk_rx[number, rows : rows + 16, :])[0:1]

    def make_factor():
        omega_mid = omega_here()

        def body(i):
            shape = (strip, strip)
            kx = (lax.broadcasted_iota(jnp.int32, shape, 0) + (mine * strip + 1)).astype(F32)
            ky = (lax.broadcasted_iota(jnp.int32, shape, 1) + (i * strip + 1)).astype(F32)
            kx = math.pi * kx / (lateral + 1)
            ky = math.pi * ky / (lateral + 1)
            q = omega_mid * omega_mid - kx * kx - ky * ky
            theta = jnp.sqrt(jnp.maximum(q, 0.0))
            damp = jnp.exp(-jnp.sqrt(jnp.maximum(-q, 0.0)))
            factor[0, :, aligned(i, strip)] = damp * jnp.cos(theta)
            factor[1, :, aligned(i, strip)] = damp * jnp.sin(theta)

        loop(0, bands, body)

    def make_first_trig():
        def body(g):
            cosine, sine = small_cos_sin(omega * slow[g].astype(F32))
            trig[0, 0, aligned(g, rows)] = cosine
            trig[0, 1, aligned(g, rows)] = sine

        loop(0, freqs, body)

    def make_trig(step):
        omega_mid = omega_here()

        def body(g):
            value = slow_mid[g // (n * n), lax.rem(g, n * n), step - 1]
            cosine, sine = small_cos_sin(omega_mid * value.astype(F32))
            trig[step, 0, aligned(g, rows)] = cosine
            trig[step, 1, aligned(g, rows)] = sine

        loop(0, freqs, body)

    def hand(u):
        return -1.0 if u == 0 else 1.0

    def to_wavenumbers(step, u):
        def shift(block, value):
            cosine = trig[step, 0, block]
            sine = trig[step, 1, block] * hand(u)
            re = value[:, 0:strip]
            im = value[:, strip:]
            shifted[u, block, 0:strip] = (re * cosine - im * sine).astype(BF16)
            shifted[u, block, strip:] = (im * cosine + re * sine).astype(BF16)

        if step == 0:

            def first(i):
                block = aligned(i, strip)
                shift(block, fields[u, block])

            loop(0, bands, first)
        else:
            wait_bytes(prx.at[u], back_recv.at[u])

            def product_back(i):
                block = aligned(i, tile)
                value = jnp.dot(table[block, :], prx[u], preferred_element_type=F32)
                keep(step - 1, u, i, value)
                shift(block, value)

            loop(0, n, product_back)
            wait_bytes(tx.at[u, :, pl.ds(0, lateral - strip)], fwd_send.at[u])

        def product(i):
            t = lax.rem(x + 1 + i, n)
            block = aligned(t, tile)
            half = jnp.dot(table[block, :], shifted[u], preferred_element_type=F32).astype(BF16)
            tx[u, 0, block] = half[:, 0:strip]
            tx[u, 1, block] = half[:, strip:]
            for p in range(2):
                j = 2 * t + p
                if step == 0:
                    dst = mid.at[u, x, :, :, aligned(c, strip)]
                    sem = mid_recv.at[u, x]
                else:
                    dst = rx.at[u, :, :, aligned(mine, strip)]
                    sem = fwd_recv.at[u]
                send(
                    tx.at[u, :, aligned(j, strip)],
                    dst,
                    fwd_send.at[u],
                    sem,
                    at(t, y, z, p),
                    j == mine,
                )

        loop(0, n, product)

    def forward(u):
        def body(i):
            q = lax.rem(x + i, n)
            wait_bytes(mid.at[u, q], mid_recv.at[u, q])
            hh = lax.rem(q + y, n)
            send(
                mid.at[u, q],
                rx.at[u, :, :, aligned(h, tile)],
                mid_send.at[u],
                fwd_recv.at[u],
                at(x, y, 2 * hh + l, c),
                hh == h,
            )

        loop(0, n, body)

    def turn(step, u):
        def product(i):
            lanes = aligned(i, tile)
            lines = rx[u].reshape(2 * strip, lateral)
            spectrum = jnp.dot(lines, table[:, lanes], preferred_element_type=F32)
            re = spectrum[0:strip]
            im = spectrum[strip:]
            cosine = factor[0, :, lanes]
            sine = factor[1, :, lanes] * hand(u)
            turned[u, 0:strip, lanes] = (re * cosine - im * sine).astype(BF16)
            turned[u, strip:, lanes] = (im * cosine + re * sine).astype(BF16)

        loop(0, n, product)
        if step > 0:
            wait_bytes(ptx.at[u, pl.ds(0, bands - 1)], back_send.at[u])
        final = step == depth - 1

        def back(i):
            t = lax.rem((h if final else x) + 1 + i, n)
            lanes = aligned(t, tile)
            partial = jnp.dot(turned[u], table[:, lanes], preferred_element_type=F32).astype(BF16)
            for p in range(2):
                j = 2 * t + p
                cols = slice(p * strip, (p + 1) * strip)
                ptx[u, j, :, 0:strip] = partial[0:strip, cols]
                ptx[u, j, :, strip:] = partial[strip:, cols]
                block = aligned(mine, strip)
                if final:
                    send(
                        ptx.at[u, j],
                        last.at[u, block],
                        last_send.at[u],
                        last_recv.at[u],
                        at(home, y, 2 * t + l, p),
                        (home == x) & (j == b),
                    )
                else:
                    send(
                        ptx.at[u, j],
                        prx.at[u, block],
                        back_send.at[u],
                        back_recv.at[u],
                        at(t, y, z, p),
                        j == mine,
                    )

        loop(0, n, back)

    def to_fields(u):
        wait_bytes(last.at[u], last_recv.at[u])

        def product(i):
            block = aligned(i, tile)
            fields[u, block] = jnp.dot(table[block, :], last[u], preferred_element_type=F32)

        loop(0, n, product)

    normalizer = 1.0 / math.sqrt(freqs)

    def keep(step, u, i, value):
        block = aligned(i, tile)
        if u == 0:
            kept[block] = value
        else:
            term = kept[block] * value
            term = (term[:, 0:strip] + term[:, strip:]) * normalizer
            per = tile // rows
            start = i * per
            plane_tx[step, start // (n * n), pl.ds(lax.rem(start, n * n), per)] = term.astype(
                BF16
            ).reshape(per, rows, strip)

    def send_terms(step):
        def body_send(i):
            g = lax.rem(y * n + x + i, n * n)
            send(
                plane_tx.at[step, :, g],
                plane_rx.at[step, x, y],
                plane_send.at[step],
                plane_recv.at[step],
                at(lax.rem(g, n), g // n, z, c),
                i == 0,
            )

        loop(0, n * n, body_send)

    def send_sums(step):
        wait_bytes(plane_rx.at[step], plane_recv.at[step])

        def body(i):
            zz = lax.rem(z + i, bands)
            total = jnp.zeros((rows, strip), F32)
            for yy in range(n):
                total += plane_rx[step, zz // 2, yy, lax.rem(zz, 2)].astype(F32)
            column_tx[step, zz] = total.astype(BF16)
            send(
                column_tx.at[step, zz],
                column_rx.at[step, z],
                up_send.at[step],
                up_recv.at[step],
                at(x, y, zz, c),
                i == 0,
            )

        loop(0, bands, body)

    def send_image():
        def term(i):
            block = aligned(i, strip)
            value = fields[0, block] * fields[1, block]
            value = (value[:, 0:strip] + value[:, strip:]) * normalizer
            image_tx[block] = value.astype(BF16)

        loop(0, bands, term)

        def body(d):
            g = lax.rem(f + d, freqs)
            remote(
                image_tx.at[aligned(g, rows)], image_rx.at[f], image_send, image_recv, {"freq": g}
            )

        loop(1, freqs, body)
        pltpu.make_async_copy(image_tx.at[aligned(f, rows)], image_rx.at[f], image_recv).start()

    make_factor()
    for load in loads:
        load.wait()
    table_load.wait()
    wait_bytes(slow, slow_recv)
    make_first_trig()
    for u in range(2):
        to_wavenumbers(0, u)
    forward(0)
    send_planes()
    wait_bytes(rx.at[0], fwd_recv.at[0])
    forward(1)
    for step in range(depth):
        for u in range(2):
            if step > 0:
                to_wavenumbers(step, u)
        for u in range(2):
            if step > 0 or u > 0:
                wait_bytes(rx.at[u], fwd_recv.at[u])
            turn(step, u)
        if step == 0:
            wait_bytes(slow_mid, slow_mid_recv)
        if step < depth - 1:
            make_trig(step + 1)
    for step in range(depth - 1):
        send_terms(step)
    for step in range(depth - 1):
        send_sums(step)
    for u in range(2):
        to_fields(u)
    send_image()
    for u in range(2):
        for k in range(2):
            bottom[0, 2 * u + k] = fields[u, :, k * strip : (k + 1) * strip]

    for step in range(depth - 1):
        wait_bytes(column_rx.at[step], up_recv.at[step])
        image[step] = jnp.sum(column_rx[step].astype(F32), axis=0)
    wait_bytes(image_rx, image_recv)
    image[depth - 1] = jnp.sum(image_rx[...].astype(F32), axis=0)

    wait_bytes(chunk_tx.at[pl.ds(0, freqs - 1)], chunk_send)
    wait_bytes(slow.at[pl.ds(0, freqs - 1)], slow_send)
    wait_bytes(column.at[pl.ds(0, bands - 1)], column_send)
    wait_bytes(slow_mid.at[:, pl.ds(0, n * n - 1)], slow_mid_send)
    for u in range(2):
        wait_bytes(mid.at[u, pl.ds(0, n - 1)], mid_send.at[u])
        wait_bytes(tx.at[u, :, pl.ds(0, lateral - strip)], fwd_send.at[u])
        wait_bytes(ptx.at[u, pl.ds(0, bands - 1)], last_send.at[u])

        @pl.when(home != x)
        def _():
            wait_bytes(ptx.at[u, 0], last_send.at[u])

    for step in range(depth - 1):
        wait_bytes(plane_tx.at[step, :, pl.ds(0, n * n - 1)], plane_send.at[step])
        wait_bytes(column_tx.at[step, pl.ds(0, bands - 1)], up_send.at[step])
    wait_bytes(image_tx.at[pl.ds(0, lateral - rows)], image_send)


def body(wavefields, slowness_store, owner_plan, freq_slot):
    freqs = lax.axis_size("freq")
    bands = lax.axis_size("band")
    lateral = wavefields.shape[2]
    depth = owner_plan.shape[0]
    n = bands // 2
    strip = lateral // bands
    rows = lateral // freqs
    dims = (freqs, bands, lateral, depth)
    smem = pl.BlockSpec(memory_space=pltpu.SMEM)
    vmem = pl.BlockSpec(memory_space=pltpu.VMEM)
    hbm = pl.BlockSpec(memory_space=pltpu.HBM)
    dma = pltpu.SemaphoreType.DMA
    return pl.pallas_call(
        functools.partial(kernel, dims),
        out_shape=(
            jax.ShapeDtypeStruct((depth, rows, strip), F32),
            jax.ShapeDtypeStruct((1, 4, lateral, strip), F32),
        ),
        in_specs=[smem, smem, hbm, hbm, hbm],
        out_specs=(vmem, vmem),
        scratch_shapes=[
            pltpu.VMEM((lateral, lateral), BF16),
            pltpu.VMEM((lateral, strip), F32),
            pltpu.VMEM((2, lateral, 2 * strip), F32),
            pltpu.VMEM((2, lateral, 2 * strip), BF16),
            pltpu.VMEM((2, 2, lateral, strip), BF16),
            pltpu.VMEM((2, n, 2, strip, 2 * strip), BF16),
            pltpu.VMEM((2, 2, strip, lateral), BF16),
            pltpu.VMEM((2, 2 * strip, lateral), BF16),
            pltpu.VMEM((2, bands, strip, 2 * strip), BF16),
            pltpu.VMEM((2, lateral, 2 * strip), BF16),
            pltpu.VMEM((2, lateral, 2 * strip), BF16),
            pltpu.VMEM((depth, 2, lateral, strip), F32),
            pltpu.VMEM((2, strip, lateral), F32),
            pltpu.VMEM((freqs, rows + 16, strip), BF16),
            pltpu.VMEM((freqs, rows + 16, strip), BF16),
            pltpu.VMEM((depth, rows, strip), BF16),
            pltpu.VMEM((freqs, rows, strip), BF16),
            pltpu.VMEM((bands, depth - 1, rows, strip), BF16),
            pltpu.VMEM((2, n * n, depth - 1, rows, strip), BF16),
            pltpu.VMEM((lateral, 2 * strip), F32),
            pltpu.VMEM((depth - 1, 2, n * n, rows, strip), BF16),
            pltpu.VMEM((depth - 1, n, n, 2, rows, strip), BF16),
            pltpu.VMEM((depth - 1, bands, rows, strip), BF16),
            pltpu.VMEM((depth - 1, bands, rows, strip), BF16),
            pltpu.VMEM((lateral, strip), BF16),
            pltpu.VMEM((freqs, rows, strip), BF16),
            dma,
            dma,
            dma,
            dma,
            dma,
            dma,
            dma,
            dma,
            dma,
            dma,
            dma,
            dma((2,)),
            dma((2,)),
            dma((2,)),
            dma((2, n)),
            dma((2,)),
            dma((2,)),
            dma((2,)),
            dma((2,)),
            dma((depth - 1,)),
            dma((depth - 1,)),
            dma((depth - 1,)),
            dma((depth - 1,)),
            dma,
            dma,
        ],
        compiler_params=pltpu.CompilerParams(
            collective_id=0, has_side_effects=True, vmem_limit_bytes=36 * 2**20
        ),
    )(owner_plan, freq_slot, jnp.asarray(sine_table(lateral)), slowness_store, wavefields)


def solution(mesh):
    in_specs = (P("freq", None, None, "band"), P("freq", None, "band"), P(), P("freq"))
    out_specs = (P(None, "freq", "band"), P("freq", None, None, "band"))
    return jax.shard_map(body, mesh=mesh, in_specs=in_specs, out_specs=out_specs, check_vma=False)
```

time: 178 us -> 145 us (0.81); the launches traced: 175 us -> 144 us
  Pallas kernels: 168 us -> 136 us
    pallas_call x1, Pallas kernels: 168 us -> 136 us  [body(): pl.pallas_call(functools.partial(kernel, dims), out_shape=(jax.ShapeDtype...]
    unnamed x6 -> x10, local copies, waits for them, and re-layouts: 5.36 us -> 6.81 us
where the time goes in v4:
time: 145 us; the launch traced here: 144 us
  Pallas kernels  136 us (94%)
  local copies, waits for them, and re-layouts  6.81 us (5%)
    pallas_call x1, Pallas kernels, body(): pl.pallas_call(functools.partial(kernel, dims), out_shape=(jax.ShapeDtype...  136 us
    unnamed x10, local copies, waits for them, and re-layouts  6.81 us

profile of v4, /device:TPU:32, one launch (start us, length us, event | category | flops | bytes accessed | tf_op | source)
XLA Modules:
  0.0 144.2 jit_solution(6785847789403310909)
XLA Ops:
  1.3 0.0 copy-start
  1.3 1.6 %copy-done = f32[1,4,1024,128]{3,2,1,0:T(8,128)S(1)} copy-done((f32[1,4,1024,128]{3,2,1,0:T(8,128)S(1)}, f32[1,4,1024,128]{3,2,1,0:T(8,128)}, u32[]{:S(2)}) %copy-start) | copy-done | bytes 2097176
  2.9 0.0 copy-start.1
  2.9 1.6 %copy-done.1 = bf16[1024,1024]{1,0:T(8,128)(2,1)S(1)} copy-done((bf16[1024,1024]{1,0:T(8,128)(2,1)S(1)}, bf16[1024,1024]{1,0:T(8,128)(2,1)}, u32[]{:S(2)}) %copy-start.1) | copy-done | bytes 2097176
  4.5 0.0 copy-start.2
  4.5 1.0 copy-done.2
  5.5 0.0 copy-start.3
  5.5 0.7 copy-done.3
  6.2 136.1 %shard_map.68 = (f32[3,32,128]{2,1,0:T(8,128)S(1)}, f32[1,4,1024,128]{3,2,1,0:T(8,128)S(1)}) custom-call(s32[3]{0:T(128)S(1)} %copy-done.3, s32[1]{0:T(128)S(6)} %copy.9.slot, bf16[1024,1024]{1,0:T(8,128)(2,1)S(1)} %copy-done.1, f32[1,1024,128]{2,1,0:T(8,128)S(1)} %copy-done.2, f32[1,4,1024,128]{3,2,1,0:T(8,128)S(1)} %copy-done), custom_call_target="tpu_custom_call" | custom-call | tf_op jit(solution)/shard_map/pallas_call | solution.py:528
  142.3 0.6 copy.10
  142.9 1.3 copy.11
Async XLA Ops:
  1.3 1.6 %copy-start = (f32[1,4,1024,128]{3,2,1,0:T(8,128)S(1)}, f32[1,4,1024,128]{3,2,1,0:T(8,128)}, u32[]{:S(2)}) copy-start(f32[1,4,1024,128]{3,2,1,0:T(8,128)} %wave.1) | copy-start | bytes 6291460
  2.9 1.6 %copy-start.1 = (bf16[1024,1024]{1,0:T(8,128)(2,1)S(1)}, bf16[1024,1024]{1,0:T(8,128)(2,1)}, u32[]{:S(2)}) copy-start(bf16[1024,1024]{1,0:T(8,128)(2,1)} %constant.2.clone.table_hbm) | copy-start | bytes 6291460
  4.5 1.0 copy-start.2
  5.5 0.7 copy-start.3

commit v5 on v4

--- a/solution.py
+++ b/solution.py
@@ -54,6 +54,8 @@
     factor,
     chunk_tx,
     chunk_rx,
+    slots_tx,
+    slots,
     select,
     slow,
     column,
@@ -70,6 +72,8 @@
     load_sem,
     chunk_send,
     chunk_recv,
+    slot_send,
+    slot_recv,
     slow_send,
     slow_recv,
     column_send,
@@ -102,7 +106,6 @@
     h, c = b // 2, lax.rem(b, 2)
     z = 2 * h + l
     home = lax.rem(h - y + n, n)
-    number = l * n * n + y * n + home
     mine = 2 * x + c
 
     def at(xx, yy, zz, cc):
@@ -131,6 +134,9 @@
             return carry
 
         lax.fori_loop(first, count, step, 0)
+
+    def spread(i):
+        return lax.rem(2 * i + i // 2, n) if n == 4 else i
 
     def aligned(i, size):
         return pl.ds(pl.multiple_of(i * size, size), size)
@@ -161,8 +167,8 @@
         load.start()
     table_load.start()
     slab_load.wait()
-    chunk_tx[:, 0:rows, :] = (slab[...] - 1.0).astype(BF16).reshape(freqs, rows, strip)
-    chunk_tx[:, rows:, :] = jnp.full((freqs, 16, strip), slot[0].astype(F32)).astype(BF16)
+    chunk_tx[...] = (slab[...] - 1.0).astype(BF16).reshape(freqs, rows, strip)
+    slots_tx[...] = jnp.full((16, strip), slot[0].astype(F32)).astype(BF16)
     pl.semaphore_wait(barrier, freqs + bands - 2)
 
     def send_chunk(d):
@@ -172,6 +178,12 @@
     loop(1, freqs, send_chunk)
     pltpu.make_async_copy(chunk_tx.at[f], chunk_rx.at[f], chunk_recv).start()
 
+    def send_slot(d):
+        remote(slots_tx, slots.at[x], slot_send, slot_recv, at(lax.rem(x + d, n), y, z, c))
+
+    loop(1, n, send_slot)
+    pltpu.make_async_copy(slots_tx, slots.at[x], slot_recv).start()
+
     def omega_of(number):
         return OMEGA_LO + (OMEGA_HI - OMEGA_LO) * (number.astype(F32) + 0.5) / freqs
 
@@ -179,7 +191,7 @@
 
     wait_bytes(chunk_rx, chunk_recv)
     for k in range(depth):
-        select[k] = chunk_rx[owner[k], 0:rows, :]
+        select[k] = chunk_rx[owner[k]]
 
     def send_slow(d):
         g = lax.rem(f + d, freqs)
@@ -218,7 +230,7 @@
         loop(0, n * n, body)
 
     def omega_here():
-        return omega_of(chunk_rx[number, rows : rows + 16, :])[0:1]
+        return omega_of(slots[home])[0:1]
 
     def make_factor():
         omega_mid = omega_here()
@@ -237,14 +249,6 @@
 
         loop(0, bands, body)
 
-    def make_first_trig():
-        def body(g):
-            cosine, sine = small_cos_sin(omega * slow[g].astype(F32))
-            trig[0, 0, aligned(g, rows)] = cosine
-            trig[0, 1, aligned(g, rows)] = sine
-
-        loop(0, freqs, body)
-
     def make_trig(step):
         omega_mid = omega_here()
 
@@ -272,6 +276,11 @@
 
             def first(i):
                 block = aligned(i, strip)
+                if u == 0:
+                    value = slow[aligned(i, strip // rows)].reshape(strip, strip)
+                    cosine, sine = small_cos_sin(omega * value.astype(F32))
+                    trig[0, 0, block] = cosine
+                    trig[0, 1, block] = sine
                 shift(block, fields[u, block])
 
             loop(0, bands, first)
@@ -288,45 +297,46 @@
             wait_bytes(tx.at[u, :, pl.ds(0, lateral - strip)], fwd_send.at[u])
 
         def product(i):
-            t = lax.rem(x + 1 + i, n)
+            t = lax.rem(x + spread(i if step == 0 else lax.rem(i + 1, n)), n)
             block = aligned(t, tile)
             half = jnp.dot(table[block, :], shifted[u], preferred_element_type=F32).astype(BF16)
             tx[u, 0, block] = half[:, 0:strip]
             tx[u, 1, block] = half[:, strip:]
-            for p in range(2):
-                j = 2 * t + p
-                if step == 0:
-                    dst = mid.at[u, x, :, :, aligned(c, strip)]
-                    sem = mid_recv.at[u, x]
-                else:
-                    dst = rx.at[u, :, :, aligned(mine, strip)]
-                    sem = fwd_recv.at[u]
-                send(
-                    tx.at[u, :, aligned(j, strip)],
-                    dst,
-                    fwd_send.at[u],
-                    sem,
-                    at(t, y, z, p),
-                    j == mine,
-                )
+            if step > 0 or u == 0:
+                send_lines(step, u, t)
 
         loop(0, n, product)
 
-    def forward(u):
-        def body(i):
-            q = lax.rem(x + i, n)
-            wait_bytes(mid.at[u, q], mid_recv.at[u, q])
-            hh = lax.rem(q + y, n)
+    def send_lines(step, u, t):
+        for p in range(2):
+            j = 2 * t + p
+            if step == 0:
+                dst = mid.at[u, x, :, :, aligned(c, strip)]
+                sem = mid_recv.at[u, x]
+            else:
+                dst = rx.at[u, :, :, aligned(mine, strip)]
+                sem = fwd_recv.at[u]
             send(
-                mid.at[u, q],
-                rx.at[u, :, :, aligned(h, tile)],
-                mid_send.at[u],
-                fwd_recv.at[u],
-                at(x, y, 2 * hh + l, c),
-                hh == h,
+                tx.at[u, :, aligned(j, strip)],
+                dst,
+                fwd_send.at[u],
+                sem,
+                at(t, y, z, p),
+                j == mine,
             )
 
-        loop(0, n, body)
+    def forward(u, i):
+        q = lax.rem(x + spread(i), n)
+        wait_bytes(mid.at[u, q], mid_recv.at[u, q])
+        hh = lax.rem(q + y, n)
+        send(
+            mid.at[u, q],
+            rx.at[u, :, :, aligned(h, tile)],
+            mid_send.at[u],
+            fwd_recv.at[u],
+            at(x, y, 2 * hh + l, c),
+            hh == h,
+        )
 
     def turn(step, u):
         def product(i):
@@ -346,7 +356,7 @@
         final = step == depth - 1
 
         def back(i):
-            t = lax.rem((h if final else x) + 1 + i, n)
+            t = lax.rem((h if final else x) + spread(lax.rem(i + 1, n)), n)
             lanes = aligned(t, tile)
             partial = jnp.dot(turned[u], table[:, lanes], preferred_element_type=F32).astype(BF16)
             for p in range(2):
@@ -376,16 +386,8 @@
 
         loop(0, n, back)
 
-    def to_fields(u):
-        wait_bytes(last.at[u], last_recv.at[u])
-
-        def product(i):
-            block = aligned(i, tile)
-            fields[u, block] = jnp.dot(table[block, :], last[u], preferred_element_type=F32)
-
-        loop(0, n, product)
-
     normalizer = 1.0 / math.sqrt(freqs)
+    per = tile // rows
 
     def keep(step, u, i, value):
         block = aligned(i, tile)
@@ -394,7 +396,6 @@
         else:
             term = kept[block] * value
             term = (term[:, 0:strip] + term[:, strip:]) * normalizer
-            per = tile // rows
             start = i * per
             plane_tx[step, start // (n * n), pl.ds(lax.rem(start, n * n), per)] = term.astype(
                 BF16
@@ -434,43 +435,62 @@
 
         loop(0, bands, body)
 
-    def send_image():
-        def term(i):
-            block = aligned(i, strip)
-            value = fields[0, block] * fields[1, block]
-            value = (value[:, 0:strip] + value[:, strip:]) * normalizer
-            image_tx[block] = value.astype(BF16)
-
-        loop(0, bands, term)
-
-        def body(d):
-            g = lax.rem(f + d, freqs)
-            remote(
-                image_tx.at[aligned(g, rows)], image_rx.at[f], image_send, image_recv, {"freq": g}
-            )
-
-        loop(1, freqs, body)
-        pltpu.make_async_copy(image_tx.at[aligned(f, rows)], image_rx.at[f], image_recv).start()
-
+    def to_fields(u):
+        wait_bytes(last.at[u], last_recv.at[u])
+
+        def product(i):
+            t = lax.rem(i + f // per, n)
+            block = aligned(t, tile)
+            value = jnp.dot(table[block, :], last[u], preferred_element_type=F32)
+            bottom[0, 2 * u, block] = value[:, 0:strip]
+            bottom[0, 2 * u + 1, block] = value[:, strip:]
+            if u == 0:
+                kept[block] = value
+                return
+            term = kept[block] * value
+            term = (term[:, 0:strip] + term[:, strip:]) * normalizer
+            image_tx[block] = term.astype(BF16)
+
+            def body(k):
+                g = t * per + k
+                send(
+                    image_tx.at[aligned(g, rows)],
+                    image_rx.at[f],
+                    image_send,
+                    image_recv,
+                    {"freq": g},
+                    g == f,
+                )
+
+            loop(0, per, body)
+
+        loop(0, n, product)
+
+    wait_bytes(slots, slot_recv)
     make_factor()
     for load in loads:
         load.wait()
     table_load.wait()
     wait_bytes(slow, slow_recv)
-    make_first_trig()
-    for u in range(2):
-        to_wavenumbers(0, u)
-    forward(0)
+    to_wavenumbers(0, 0)
+    forward(0, 0)
+    to_wavenumbers(0, 1)
+    send_lines(0, 1, x)
+    forward(1, 0)
+
+    def alternate(i):
+        forward(0, i)
+        send_lines(0, 1, lax.rem(x + spread(i), n))
+
+    loop(1, n, alternate)
+    loop(1, n, functools.partial(forward, 1))
     send_planes()
-    wait_bytes(rx.at[0], fwd_recv.at[0])
-    forward(1)
     for step in range(depth):
         for u in range(2):
             if step > 0:
                 to_wavenumbers(step, u)
         for u in range(2):
-            if step > 0 or u > 0:
-                wait_bytes(rx.at[u], fwd_recv.at[u])
+            wait_bytes(rx.at[u], fwd_recv.at[u])
             turn(step, u)
         if step == 0:
             wait_bytes(slow_mid, slow_mid_recv)
@@ -478,15 +498,10 @@
             make_trig(step + 1)
     for step in range(depth - 1):
         send_terms(step)
+    to_fields(0)
     for step in range(depth - 1):
         send_sums(step)
-    for u in range(2):
-        to_fields(u)
-    send_image()
-    for u in range(2):
-        for k in range(2):
-            bottom[0, 2 * u + k] = fields[u, :, k * strip : (k + 1) * strip]
-
+    to_fields(1)
     for step in range(depth - 1):
         wait_bytes(column_rx.at[step], up_recv.at[step])
         image[step] = jnp.sum(column_rx[step].astype(F32), axis=0)
@@ -494,6 +509,7 @@
     image[depth - 1] = jnp.sum(image_rx[...].astype(F32), axis=0)
 
     wait_bytes(chunk_tx.at[pl.ds(0, freqs - 1)], chunk_send)
+    wait_bytes(slots.at[pl.ds(0, n - 1)], slot_send)
     wait_bytes(slow.at[pl.ds(0, freqs - 1)], slow_send)
     wait_bytes(column.at[pl.ds(0, bands - 1)], column_send)
     wait_bytes(slow_mid.at[:, pl.ds(0, n * n - 1)], slow_mid_send)
@@ -547,8 +563,10 @@
             pltpu.VMEM((2, lateral, 2 * strip), BF16),
             pltpu.VMEM((depth, 2, lateral, strip), F32),
             pltpu.VMEM((2, strip, lateral), F32),
-            pltpu.VMEM((freqs, rows + 16, strip), BF16),
-            pltpu.VMEM((freqs, rows + 16, strip), BF16),
+            pltpu.VMEM((freqs, rows, strip), BF16),
+            pltpu.VMEM((freqs, rows, strip), BF16),
+            pltpu.VMEM((16, strip), BF16),
+            pltpu.VMEM((n, 16, strip), BF16),
             pltpu.VMEM((depth, rows, strip), BF16),
             pltpu.VMEM((freqs, rows, strip), BF16),
             pltpu.VMEM((bands, depth - 1, rows, strip), BF16),
@@ -560,6 +578,8 @@
             pltpu.VMEM((depth - 1, bands, rows, strip), BF16),
             pltpu.VMEM((lateral, strip), BF16),
             pltpu.VMEM((freqs, rows, strip), BF16),
+            dma,
+            dma,
             dma,
             dma,
             dma,
@@ -587,7 +607,7 @@
             dma,
         ],
         compiler_params=pltpu.CompilerParams(
-            collective_id=0, has_side_effects=True, vmem_limit_bytes=36 * 2**20
+            collective_id=0, has_side_effects=True, vmem_limit_bytes=51 * 2**20
         ),
     )(owner_plan, freq_slot, jnp.asarray(sine_table(lateral)), slowness_store, wavefields)
 

time: 145 us -> 134 us (0.924)
  Pallas kernels: 136 us -> 127 us
  local copies, waits for them, and re-layouts: 6.81 us -> 3.63 us
    pallas_call x1, Pallas kernels: 136 us -> 127 us  [body(): pl.pallas_call(functools.partial(kernel, dims), out_shape=(jax.ShapeDtype...]
    unnamed x10 -> x6, local copies, waits for them, and re-layouts: 6.81 us -> 3.63 us
where the time goes in v5:
time: 134 us; the launch traced here: 132 us
  Pallas kernels  127 us (95%)
  local copies, waits for them, and re-layouts  3.63 us (3%)
    pallas_call x1, Pallas kernels, body(): pl.pallas_call(functools.partial(kernel, dims), out_shape=(jax.ShapeDtype...  127 us
    unnamed x6, local copies, waits for them, and re-layouts  3.63 us

profile of v5, /device:TPU:32, one launch (start us, length us, event | category | flops | bytes accessed | tf_op | source)
XLA Modules:
  0.0 132.1 jit_solution(12343105316564859970)
XLA Ops:
  1.3 0.0 copy-start
  1.3 1.0 copy-done
  2.3 0.0 copy-start.1
  2.3 0.7 copy-done.1
  3.0 127.2 %shard_map.68 = (f32[3,32,128]{2,1,0:T(8,128)S(1)}, f32[1,4,1024,128]{3,2,1,0:T(8,128)S(1)}) custom-call(s32[3]{0:T(128)S(1)} %copy-done.1, s32[1]{0:T(128)S(6)} %copy.9.slot, bf16[1024,1024]{1,0:T(8,128)(2,1)} %constant.2.clone.table_hbm, f32[1,1024,128]{2,1,0:T(8,128)S(1)} %copy-done, f32[1,4,1024,128]{3,2,1,0:T(8,128)} %wave.1), custom_call_target="tpu_custom_call" | custom-call | tf_op jit(solution)/shard_map/pallas_call | solution.py:544
  130.2 0.6 copy.10
  130.8 1.3 copy.11
Async XLA Ops:
  1.3 1.0 copy-start
  2.3 0.7 copy-start.1

commit v6 on v5

--- a/solution.py
+++ b/solution.py
@@ -309,7 +309,7 @@
 
     def send_lines(step, u, t):
         for p in range(2):
-            j = 2 * t + p
+            j = 2 * t + lax.rem(p + c, 2)
             if step == 0:
                 dst = mid.at[u, x, :, :, aligned(c, strip)]
                 sem = mid_recv.at[u, x]
@@ -321,7 +321,7 @@
                 dst,
                 fwd_send.at[u],
                 sem,
-                at(t, y, z, p),
+                at(t, y, z, lax.rem(j, 2)),
                 j == mine,
             )
 
@@ -364,6 +364,9 @@
                 cols = slice(p * strip, (p + 1) * strip)
                 ptx[u, j, :, 0:strip] = partial[0:strip, cols]
                 ptx[u, j, :, strip:] = partial[strip:, cols]
+            for p in range(2):
+                core = lax.rem(p + c, 2)
+                j = 2 * t + core
                 block = aligned(mine, strip)
                 if final:
                     send(
@@ -371,7 +374,7 @@
                         last.at[u, block],
                         last_send.at[u],
                         last_recv.at[u],
-                        at(home, y, 2 * t + l, p),
+                        at(home, y, 2 * t + l, core),
                         (home == x) & (j == b),
                     )
                 else:
@@ -380,7 +383,7 @@
                         prx.at[u, block],
                         back_send.at[u],
                         back_recv.at[u],
-                        at(t, y, z, p),
+                        at(t, y, z, core),
                         j == mine,
                     )
 
@@ -466,8 +469,6 @@
 
         loop(0, n, product)
 
-    wait_bytes(slots, slot_recv)
-    make_factor()
     for load in loads:
         load.wait()
     table_load.wait()
@@ -485,6 +486,8 @@
     loop(1, n, alternate)
     loop(1, n, functools.partial(forward, 1))
     send_planes()
+    wait_bytes(slots, slot_recv)
+    make_factor()
     for step in range(depth):
         for u in range(2):
             if step > 0:

time: 134 us -> 135 us (level)
  no operation moved by 1% of the time
where the time goes in v6:
time: 135 us; the launch traced here: 133 us
  Pallas kernels  128 us (95%)
  local copies, waits for them, and re-layouts  3.63 us (3%)
    pallas_call x1, Pallas kernels, body(): pl.pallas_call(functools.partial(kernel, dims), out_shape=(jax.ShapeDtype...  128 us
    unnamed x6, local copies, waits for them, and re-layouts  3.63 us

profile of v6, /device:TPU:32, one launch (start us, length us, event | category | flops | bytes accessed | tf_op | source)
XLA Modules:
  0.0 133.0 jit_solution(15176621943263286508)
XLA Ops:
  1.3 0.0 copy-start
  1.3 1.0 copy-done
  2.3 0.0 copy-start.1
  2.3 0.7 copy-done.1
  3.0 128.1 %shard_map.68 = (f32[3,32,128]{2,1,0:T(8,128)S(1)}, f32[1,4,1024,128]{3,2,1,0:T(8,128)S(1)}) custom-call(s32[3]{0:T(128)S(1)} %copy-done.1, s32[1]{0:T(128)S(6)} %copy.9.slot, bf16[1024,1024]{1,0:T(8,128)(2,1)} %constant.2.clone.table_hbm, f32[1,1024,128]{2,1,0:T(8,128)S(1)} %copy-done, f32[1,4,1024,128]{3,2,1,0:T(8,128)} %wave.1), custom_call_target="tpu_custom_call" | custom-call | tf_op jit(solution)/shard_map/pallas_call | solution.py:547
  131.1 0.6 copy.10
  131.7 1.3 copy.11
Async XLA Ops:
  1.3 1.0 copy-start
  2.3 0.7 copy-start.1
